TPU v7x, 256 devices: a whole 4x4x8 slice. The times are simulated.
256 devices in a mesh: seq: 64 (over z, x, core), head: 4 (over y).
Axes of the slice: x: 4, y: 4, z: 8, core: 2. Of those that a mesh axis runs over, the one named last changes fastest.
Arguments:
- queries: bfloat16 [16384, 4096], P('seq', 'head'), may hold values from -6 to 6
- key_vectors: bfloat16 [16384, 2, 4096], P('seq', None, 'head'), may hold values from -6 to 6
- values: bfloat16 [16384, 2, 4096], P('seq', None, 'head'), may hold values from -0.59765625 to 0.59765625
- beta_rates: float32 [16384, 64], P('seq', 'head'), may hold values from 0 to 2, as said below
- log_gate: float32 [16384, 32], P('seq', 'head'), may hold values from -0.7 to 0, as said below
- norm_gain: float32 [128], replicated, may hold values from 0.1 to 1.9
- out_weight: bfloat16 [4096, 4096], P('head'), may hold values from -0.09375 to 0.09375
- decode_owner: int32 [2, 32], P(None, 'head'), may hold values from 0 to 63, as said below
Outputs:
- mixed: bfloat16 [16384, 4096], P(('seq', 'head'))
- decode_states: float32 [64, 32, 128, 128], P('seq', 'head')
Inputs may be any that keep to these rules, and one draw needn't show every extreme that they name: `beta_rates`: every rate lies strictly between 0 and 2. `log_gate`: every entry is negative. `decode_owner`: every decode device owns at least one head.
All inputs are finite; a program needn't handle non-finite values.
Results may differ from a plain program's by a relative error of at most 0.0065.
Values sent between devices are 32-bit elements; how exact they have to be, the bound alone decides.
A program may use at most 192 MiB of HBM per device.

v0:
```python
import jax
import jax.numpy as jnp
from jax import lax
from jax.sharding import PartitionSpec as P

BLOCK = 64


EXACT_PRECISION = lax.Precision.HIGHEST


def carried_in(value, axis, join, neutral):
    count, mine = (lax.axis_size(axis), lax.axis_index(axis))
    pieces = jax.tree.map(lambda part: lax.all_gather(part, axis), value)
    subtotal = jax.tree.map(
        lambda part, zero: jnp.full_like(part, 0) + jnp.asarray(zero, part.dtype), value, neutral
    )

    def lap(position, subtotal):
        longer = join(subtotal, jax.tree.map(lambda part: part[position], pieces))
        return jax.tree.map(lambda new, old: jnp.where(position < mine, new, old), longer, subtotal)

    return lax.fori_loop(0, count - 1, lap, subtotal)


def from_root(value, axis, source):
    kept = jnp.where(lax.axis_index(axis) == source, value, 0).astype(value.dtype)
    return lax.psum(kept, axis)


def product(left_factor, right_factor):
    return jnp.einsum("ywc,ycp->ywp", left_factor, right_factor, precision=EXACT_PRECISION)


def prepare(queries, key_vectors, values, beta_rates, log_gate):
    token_count = queries.shape[0]
    head_count = log_gate.shape[1]
    head_width = queries.shape[1] // head_count
    block_count = token_count // BLOCK
    row_span = 2 * BLOCK
    key_f = key_vectors.astype(jnp.float32).reshape(token_count, 2, head_count, head_width)
    key_unit = key_f * lax.rsqrt(jnp.sum(key_f * key_f, -1, keepdims=True) + 1e-06)
    key_unit = key_unit.reshape(block_count, BLOCK, 2, head_count, head_width).transpose(
        0, 3, 1, 2, 4
    )
    key_unit = key_unit.reshape(block_count, head_count, row_span, head_width)
    value_f = values.astype(jnp.float32).reshape(block_count, BLOCK, 2, head_count, head_width)
    value_f = value_f.transpose(0, 3, 1, 2, 4).reshape(
        block_count, head_count, row_span, head_width
    )
    query_f = (
        queries.astype(jnp.float32)
        .reshape(block_count, BLOCK, head_count, head_width)
        .transpose(0, 2, 1, 3)
    )
    rates = beta_rates.reshape(block_count, BLOCK, head_count, 2).transpose(0, 2, 1, 3)
    rates = rates.reshape(block_count, head_count, row_span)
    decay = jnp.stack([log_gate, jnp.zeros_like(log_gate)], -1).reshape(
        block_count, BLOCK, head_count, 2
    )
    decay = decay.transpose(0, 2, 1, 3).reshape(block_count, head_count, row_span)
    running = jnp.cumsum(decay, -1)
    closing = running[..., -1:]
    later_row = lax.broadcasted_iota(jnp.int32, (row_span, row_span), 0)
    earlier_row = lax.broadcasted_iota(jnp.int32, (row_span, row_span), 1)
    below = later_row > earlier_row
    spread_gap = running[..., :, None] - running[..., None, :]
    weights = jnp.where(below, jnp.exp(jnp.where(below, spread_gap, 0.0)), 0.0)
    gram = jnp.einsum("bhrk,bhsk->bhrs", key_unit, key_unit, precision=EXACT_PRECISION)
    system = jnp.eye(row_span, dtype=jnp.float32) + rates[..., :, None] * weights * gram
    right_side = jnp.concatenate(
        [rates[..., None] * value_f, (rates * jnp.exp(running))[..., None] * key_unit], -1
    )
    solved = jax.scipy.linalg.solve_triangular(system, right_side, lower=True, unit_diagonal=True)
    pseudo = solved[..., :head_width]
    wy_rows = solved[..., head_width:]
    key_decayed = jnp.exp(closing - running)[..., None] * key_unit
    identity_rows = jnp.eye(head_width, dtype=jnp.float32)
    transition = jnp.exp(closing)[..., None] * identity_rows - jnp.einsum(
        "bhrk,bhrj->bhkj", key_decayed, wy_rows, precision=EXACT_PRECISION
    )
    contrib = jnp.einsum("bhrk,bhrv->bhkv", key_decayed, pseudo, precision=EXACT_PRECISION)
    query_running = running[..., 1::2]
    query_row = lax.broadcasted_iota(jnp.int32, (BLOCK, row_span), 0)
    seen_row = lax.broadcasted_iota(jnp.int32, (BLOCK, row_span), 1)
    visible = seen_row <= 2 * query_row + 1
    query_gap = query_running[..., :, None] - running[..., None, :]
    query_weights = jnp.where(visible, jnp.exp(jnp.where(visible, query_gap, 0.0)), 0.0)
    scores = (
        jnp.einsum("bhtk,bhsk->bhts", query_f, key_unit, precision=EXACT_PRECISION) * query_weights
    )
    local_out = jnp.einsum("bhts,bhsv->bhtv", scores, pseudo, precision=EXACT_PRECISION)
    reach_span = jnp.exp(query_running)[..., None] * query_f - jnp.einsum(
        "bhts,bhsk->bhtk", scores, wy_rows, precision=EXACT_PRECISION
    )
    return (transition, contrib, reach_span, local_out)


def run_chain(parts, start_state, emit_out, track_prod):
    head_count, head_width = (start_state.shape[0], start_state.shape[1])
    identity = jnp.broadcast_to(
        jnp.eye(head_width, dtype=jnp.float32), (head_count, head_width, head_width)
    )

    def advance(carried, inputs):
        current_state, totals = carried
        transition, contrib, reach_span, local_out = inputs
        emitted_out = None
        if emit_out:
            emitted_out = local_out + jnp.einsum(
                "ozj,oja->oza", reach_span, current_state, precision=EXACT_PRECISION
            )
        emitted_prod = None
        new_totals = product(transition, totals) if track_prod else totals
        return (
            (product(transition, current_state) + contrib, new_totals),
            (emitted_out, emitted_prod),
        )

    return lax.scan(advance, (start_state, identity), parts)


def per_device(
    queries, key_vectors, values, beta_rates, log_gate, norm_gain, out_weight, decode_owner
):
    parts = prepare(queries, key_vectors, values, beta_rates, log_gate)
    head_count = log_gate.shape[1]
    head_width = norm_gain.shape[0]
    zero_state = jnp.zeros((head_count, head_width, head_width), jnp.float32)
    identity = jnp.broadcast_to(
        jnp.eye(head_width, dtype=jnp.float32), (head_count, head_width, head_width)
    )
    (own_state, own_prod), _ = run_chain(parts, zero_state, False, True)

    def combine(earlier, later):
        return (product(later[0], earlier[0]), product(later[0], earlier[1]) + later[1])

    prefix = carried_in((own_prod, own_state), "seq", combine, (identity, zero_state))
    incoming = prefix[1]
    _, (attended, _) = run_chain(parts, incoming, True, False)
    scaling = lax.rsqrt(jnp.mean(attended * attended, -1, keepdims=True) + 1e-06)
    normed = (attended * scaling * norm_gain).astype(jnp.bfloat16)
    token_count = queries.shape[0]
    normed = normed.transpose(0, 2, 1, 3).reshape(token_count, head_count * head_width)
    mixed = lax.psum_scatter(
        jnp.dot(normed, out_weight, preferred_element_type=jnp.float32),
        "head",
        scatter_dimension=0,
        tiled=True,
    ).astype(jnp.bfloat16)
    final_state = product(own_prod, incoming) + own_state
    shared = from_root(final_state, "seq", lax.axis_size("seq") - 1)
    position = lax.axis_index("seq")
    owned = jnp.any(decode_owner == position, axis=0)
    decode_states = jnp.where(owned[:, None, None], shared, 0.0)[None]
    return (mixed, decode_states)


def solution(mesh):
    in_specs = (
        P("seq", "head"),
        P("seq", None, "head"),
        P("seq", None, "head"),
        P("seq", "head"),
        P("seq", "head"),
        P(),
        P("head", None),
        P(None, "head"),
    )
    out_specs = (P(("seq", "head"), None), P("seq", "head", None, None))
    return jax.shard_map(
        per_device, mesh=mesh, in_specs=in_specs, out_specs=out_specs, check_vma=False
    )
```

profile of v0, /device:TPU:1, one launch (start us, length us, event | category | flops | bytes accessed | tf_op | source)
XLA Modules:
  0.0 1052.2 jit_solution(14983207912612248774)
XLA Ops:
  12.4 2.5 copy.51
  14.9 2.7 reshape.96
  19.2 2.9 mul.119
  24.7 4.4 copy_multiply_fusion
  29.1 5.8 add_bitcast_fusion
  34.9 315.8 %custom-call.4 = f32[4,8,1,128,128]{3,4,2,1,0:T(8,128)} custom-call(f32[4,8,1,128,128]{4,3,2,1,0:T(8,128)} %add_bitcast_fusion), custom_call_target="InvertDiagBlocksLowerTriangular" | custom-call | tf_op jit(solution)/shard_map/jit(_solve_triangular)/vmap(vmap())/triangular_solve | solution.py:74
  350.8 2.8 broadcast_multiply_fusion
  353.6 3.8 fusion.27
  357.4 5.5 fusion.34
  362.9 5.8 multiply_subtract_fusion
  368.7 15.9 %while.43 = (s32[]{:T(128)}, f32[8,128,128]{2,1,0:T(8,128)S(1)}, f32[8,128,128]{2,1,0:T(8,128)S(1)}, f32[4,8,128,128]{3,2,1,0:T(8,128)}, f32[4,8,128,128]{3,2,1,0:T(8,128)}) while((s32[]{:T(128)}, f32[8,128,128]{2,1,0:T(8,128)S(1)}, f32[8,128,128]{2,1,0:T(8,128)S(1)}, f32[4,8,128,128]{3,2,1,0:T(8,128)}, ...), condition=%wide.region_3.4_spmd.clone.clone, body=%wide.region_2.3_spmd.clone.sunk.clone | while | flops 402915328 | bytes 14157422 | solution.py:120
  387.9 2.3 fusion.49
  390.1 3.7 fusion.32
  393.9 3.1 fusion.46
  397.0 135.3 %all-gather.5.cloned.1.call-done = f32[512,128,128]{2,1,0:T(8,128)} async-done(((f32[8,128,128]{2,1,0:T(8,128)}), f32[512,128,128]{2,1,0:T(8,128)}) %all-gather.5.cloned.1.call-update) | async-done | bytes 33554448 | tf_op jit(solution)/shard_map/all_gather | solution.py:14
  532.3 142.9 %all-gather.7.cloned.1.call-done = f32[512,128,128]{2,1,0:T(8,128)} async-done(((f32[8,128,128]{2,1,0:T(8,128)}), f32[512,128,128]{2,1,0:T(8,128)}) %all-gather.7.cloned.1.call-update) | async-done | bytes 33554448 | tf_op jit(solution)/shard_map/all_gather | solution.py:14
  675.2 122.7 %while.44 = (s32[]{:T(128)}, f32[8,128,128]{2,1,0:T(8,128)S(1)}, s32[]{:T(128)}, f32[64,8,128,128]{3,2,1,0:T(8,128)}, f32[64,8,128,128]{3,2,1,0:T(8,128)}) while((s32[]{:T(128)}, f32[8,128,128]{2,1,0:T(8,128)S(1)}, s32[]{:T(128)}, f32[64,8,128,128]{3,2,1,0:T(8,128)}, f32[64,8,128,128]{3,2,1,0:T(8,128)}) %tuple.100), condition=%wide.region_5.6_spmd.clone.clone, body=%wide.region_4.5_spmd.clone.sunk.clone | while | flops 201850880 | bytes 3672663 | solution.py:23
  675.2 2.0 fusion.111
  677.2 1.9 fusion.111
  679.2 1.9 fusion.111
  681.1 1.9 fusion.111
  683.1 1.9 fusion.111
  685.0 1.9 fusion.111
  687.0 1.9 fusion.111
  688.9 1.9 fusion.111
  692.8 1.9 fusion.111
  694.7 1.9 fusion.111
  696.7 1.9 fusion.111
  698.6 1.9 fusion.111
  700.6 1.9 fusion.111
  702.5 1.9 fusion.111
  704.5 1.9 fusion.111
  706.4 1.9 fusion.111
  708.4 1.9 fusion.111
  710.3 1.9 fusion.111
  712.3 1.9 fusion.111
  714.2 1.9 fusion.111
  716.2 1.9 fusion.111
  718.1 1.9 fusion.111
  720.1 1.9 fusion.111
  722.0 1.9 fusion.111
  724.0 1.9 fusion.111
  725.9 1.9 fusion.111
  727.8 1.9 fusion.111
  729.8 1.9 fusion.111
  731.7 1.9 fusion.111
  733.7 1.9 fusion.111
  737.6 1.9 fusion.111
  743.4 1.9 fusion.111
  753.2 1.9 fusion.111
  762.9 1.9 fusion.111
  772.6 1.9 fusion.111
  782.4 1.9 fusion.111
  792.1 1.9 fusion.111
  799.3 16.7 %while.42 = (s32[]{:T(128)}, f32[8,128,128]{2,1,0:T(8,128)S(1)}, f32[4,8,64,128]{3,2,1,0:T(8,128)}, f32[4,8,128,128]{3,2,1,0:T(8,128)}, f32[4,8,128,128]{3,2,1,0...) while((s32[]{:T(128)}, f32[8,128,128]{2,1,0:T(8,128)S(1)}, ...), condition=%wide.region_7.8_spmd.clone, body=%wide.region_6.7_spmd.sunk.clone | while | flops 302186496 | bytes 4458581 | solution.py:120
  799.4 2.3 fusion.103
  803.6 2.3 fusion.103
  807.7 2.3 fusion.103
  811.9 2.3 fusion.103
  818.7 7.7 fusion.54
  827.0 165.3 %all-reduce.3.cloned.1.call-done = f32[8,128,128]{2,1,0:T(8,128)} async-done(((f32[8,128,128]{2,1,0:T(8,128)}), f32[8,128,128]{2,1,0:T(8,128)}) %all-reduce.3.cloned.1.call-update) | async-done | bytes 524304 | tf_op jit(solution)/shard_map/psum | solution.py:28
  992.4 1.9 select_bitcast_fusion
  994.3 49.3 %reduce-scatter.2.cloned.1.call-done = f32[64,4096]{1,0:T(8,128)} async-done(((f32[256,4096]{1,0:T(8,128)}), f32[64,4096]{1,0:T(8,128)}) %reduce-scatter.2.cloned.1.call-update) | async-done | bytes 1048592 | tf_op jit(solution)/shard_map/reduce_scatter | solution.py:145
  1043.6 2.1 convert_element_type.29
  (185 shorter events, 91.3 us)
Async XLA Ops:
  7.2 525.1 %all-gather.5.cloned.1.call-start = ((), (), s32[]{:S(2)}) async-start(), calls=%async_computation.3 | async-start | bytes 34078720 | tf_op jit(solution)/shard_map/all_gather | solution.py:14
  14.9 2.7 copy-start.7
  350.8 2.8 copy-start.9
  357.4 5.5 copy-start.1
  368.8 1.6 copy-start
  372.7 1.6 copy-start
  376.7 1.6 copy-start
  380.7 1.6 copy-start
  384.6 0.8 copy-start.3
  384.6 1.0 copy-start.5
  385.4 289.7 %all-gather.7.cloned.1.call-start = ((), (), s32[]{:S(2)}) async-start(), calls=%async_computation.4 | async-start | bytes 34078720 | tf_op jit(solution)/shard_map/all_gather | solution.py:14
  386.2 606.2 %all-reduce.3.cloned.1.call-start = ((), (), s32[]{:S(2)}) async-start(), calls=%async_computation.2 | async-start | bytes 1048576 | tf_op jit(solution)/shard_map/psum | solution.py:28
  390.1 3.8 copy-start.2
  675.2 122.7 %copy-start.4 = (f32[8,128,128]{2,1,0:T(8,128)S(1)}, f32[8,128,128]{2,1,0:T(8,128)}, u32[]{:S(2)}) copy-start(f32[8,128,128]{2,1,0:T(8,128)} %copy-done.3) | copy-start | bytes 1572868
  675.2 122.7 %copy-start.6 = (f32[8,128,128]{2,1,0:T(8,128)S(1)}, f32[8,128,128]{2,1,0:T(8,128)}, u32[]{:S(2)}) copy-start(f32[8,128,128]{2,1,0:T(8,128)} %copy-done.5) | copy-start | bytes 1572868
  799.3 18.6 %copy-start.11 = (f32[128]{0:T(128)S(1)}, f32[128]{0:T(128)}, u32[]{:S(2)}) copy-start(f32[128]{0:T(128)} %param.19) | copy-start | bytes 1540
  816.0 1.9 copy-start.8
  816.1 227.5 %reduce-scatter.2.cloned.1.call-start = ((), (), s32[]{:S(2)}) async-start(), calls=%async_computation.1 | async-start | bytes 5242880 | tf_op jit(solution)/shard_map/reduce_scatter | solution.py:145
  826.3 0.7 copy-start.10
Sparse Core Ops, SparseCore 0:
  385.6 146.6 all-gather.4
  535.6 139.4 all-gather.6
  816.2 176.1 all-reduce.2
  994.8 48.7 reduce-scatter.1
where the time goes:
time: 1050 us
  waiting for transfers between devices  493 us (47%)
  other arithmetic  333 us (32%)
  matrix products  183 us (17%)
  local copies, waits for them, and re-layouts  25.7 us (2%)
  between operations  14.1 us (1%)
    another operation x2, other arithmetic, prepare(): jax.scipy.linalg.solve_triangular(system, right_side, lower=True, unit_di...  316 us
    all_gather x2, waiting for transfers between devices, carried_in(): pieces = jax.tree.map(lambda part: lax.all_gather(part, axis), value)  278 us
    psum x1, waiting for transfers between devices, from_root(): return lax.psum(kept, axis)  165 us
    dot_general x76, matrix products, product(): jnp.einsum('ywc,ycp->ywp', left_factor, right_factor, precision=EXACT_PRE...  136 us
    reduce_scatter x1, waiting for transfers between devices, per_device(): lax.psum_scatter(jnp.dot(normed, out_weight, preferred_element_type=jnp.f...  49.3 us
  transfers between devices with their start and end apart: 4, of which 4 were waited for; matrix products, arithmetic and copies ran while one was open for 2% of the time, Pallas kernels for 0%

commit v1 on v0

v1 whole, which is shorter than its diff:
```python
import functools
import jax
import jax.numpy as jnp
from jax import lax
from jax.experimental import pallas as pl
from jax.experimental.pallas import tpu as pltpu
from jax.sharding import PartitionSpec as P

K = 128
TB = 64
ROWS = 2 * TB
SUB = 8
F32 = jnp.float32
BF16 = jnp.bfloat16


def split(x):
    hi = x.astype(BF16)
    return hi, (x - hi.astype(F32)).astype(BF16)


def bdot(a, b):
    if a.ndim == 2:
        return lax.dot_general(a, b, (((1,), (0,)), ((), ())), preferred_element_type=F32)
    return lax.dot_general(a, b, (((2,), (1,)), ((0,), (0,))), preferred_element_type=F32)


def mm3(a, b):
    ah, al = a if isinstance(a, tuple) else split(a)
    bh, bl = b if isinstance(b, tuple) else split(b)
    wide = jnp.concatenate([ah, al], axis=-1)
    tall = jnp.concatenate([bh, bh], axis=-2)
    return bdot(wide, tall) + bdot(ah, bl)


def iota(shape, dim):
    return lax.broadcasted_iota(jnp.int32, shape, dim)


def transition_kernel(nb, q_ref, k_ref, v_ref, beta_ref, gate_ref, sp_ref, r_ref, o_ref, run_scr, row_scr):
    h = pl.program_id(0)
    tokens = nb * TB

    @pl.when(h == 0)
    def _():
        gate = gate_ref[...]
        t_i, s_i = iota((tokens, tokens), 0), iota((tokens, tokens), 1)
        same = (t_i // TB) == (s_i // TB)
        upto = jnp.where(same & (s_i <= t_i), 1.0, 0.0).astype(F32)
        run_scr[...] = lax.dot_general(
            upto, gate, (((1,), (0,)), ((), ())), precision=lax.Precision.HIGHEST, preferred_element_type=F32
        )
        t_j, l_j = iota((tokens, nb * ROWS), 0), iota((tokens, nb * ROWS), 1)
        spread = jnp.where(
            ((t_j // TB) == (l_j // ROWS)) & ((t_j % TB) <= (l_j % TB)), 1.0, 0.0
        ).astype(F32)
        row_scr[...] = lax.dot_general(
            gate, spread, (((0,), (0,)), ((), ())), precision=lax.Precision.HIGHEST, preferred_element_type=F32
        )

    heads = gate_ref.shape[1]
    lane_h = iota((tokens, heads), 1)
    run = jnp.sum(jnp.where(lane_h == h, run_scr[...], 0.0), axis=1, keepdims=True).reshape(nb, TB, 1)
    lane_b = iota((tokens, 2 * heads), 1)
    beta = beta_ref[...]
    beta0 = jnp.sum(jnp.where(lane_b == 2 * h, beta, 0.0), axis=1, keepdims=True).reshape(nb, TB, 1)
    beta1 = jnp.sum(jnp.where(lane_b == 2 * h + 1, beta, 0.0), axis=1, keepdims=True).reshape(nb, TB, 1)
    rates = jnp.concatenate([beta0, beta1], axis=1)
    run_rows = jnp.concatenate([run, run], axis=1)
    lane_run = jnp.sum(
        jnp.where(iota((heads, nb * ROWS), 0) == h, row_scr[...], 0.0), axis=0, keepdims=True
    )
    run_lane = jnp.stack([lane_run[:, b * ROWS:(b + 1) * ROWS] for b in range(nb)], axis=0)
    closing = run_lane[:, :, ROWS - 1:ROWS]

    def unit(x):
        x = x.astype(F32)
        return x * lax.rsqrt(jnp.sum(x * x, axis=-1, keepdims=True) + 1e-6)

    k0 = unit(k_ref[0]).reshape(nb, TB, K)
    k1 = unit(k_ref[1]).reshape(nb, TB, K)
    key = jnp.concatenate([k0, k1], axis=1)
    val = jnp.concatenate(
        [v_ref[0].astype(F32).reshape(nb, TB, K), v_ref[1].astype(F32).reshape(nb, TB, K)], axis=1
    )
    query = q_ref[...].astype(F32).reshape(nb, TB, K)
    key_t = jnp.stack([key[b].T for b in range(nb)], axis=0)
    kth, ktl = split(key_t)
    gram = mm3(jnp.concatenate([key, query], axis=1), (kth, ktl))

    row_t, lane_t = iota((TB, ROWS), 0), iota((TB, ROWS), 1) % TB
    seen = lane_t <= row_t
    decay = jnp.where(seen, jnp.exp(jnp.where(seen, run - run_lane, 0.0)), 0.0)
    scores = gram[:, ROWS:] * decay
    r_i, s_i = iota((ROWS, ROWS), 0), iota((ROWS, ROWS), 1)
    r_t, s_t = r_i % TB, s_i % TB
    below = (r_t > s_t) | ((r_t == s_t) & (r_i > s_i))
    system = jnp.where(below, rates * jnp.concatenate([decay, decay], axis=1) * gram[:, :ROWS], 0.0)

    near = (r_t // SUB) == (s_t // SUB)
    folded = jnp.sum(
        jnp.where(near, system, 0.0).reshape(nb, 2, TB // SUB, SUB, ROWS), axis=2
    ).reshape(nb * 2 * SUB, ROWS)
    e_i, e_l = iota((2 * SUB, ROWS), 0), iota((2 * SUB, ROWS), 1)
    eye = jnp.where(((e_i // SUB) == (e_l // TB)) & ((e_i % SUB) == (e_l % SUB)), 1.0, 0.0).astype(F32)
    inv = jnp.broadcast_to(eye, (nb, 2 * SUB, ROWS))
    base = (iota((nb * 2 * SUB, ROWS), 1) % TB) // SUB * SUB
    for i in range(SUB):
        for j in range(2):
            if i == SUB - 1 and j == 1:
                continue
            factor = jnp.take_along_axis(folded, base + (j * TB + i), axis=1, mode="promise_in_bounds")
            factor = factor.reshape(nb, 2 * SUB, ROWS)
            at = j * SUB + i
            inv = inv - factor * inv[:, at:at + 1, :]
    solve = jnp.broadcast_to(
        inv.reshape(nb, 2, 1, SUB, ROWS), (nb, 2, TB // SUB, SUB, ROWS)
    ).reshape(nb, ROWS, ROWS)
    solve = jnp.where(near, solve, 0.0)
    size = SUB
    while size < TB:
        pair = ((r_t // (2 * size)) == (s_t // (2 * size))) & ((r_t // size) > (s_t // size))
        parts = split(solve)
        solve = solve - mm3(parts, mm3(jnp.where(pair, system, 0.0), parts))
        size *= 2

    grown = jnp.exp(run_rows)
    right = jnp.concatenate([rates * val, (rates * grown) * key], axis=2)
    rows = split(mm3(solve, right))
    key_decayed = key_t * jnp.exp(closing - run_lane)
    z = mm3(jnp.concatenate([key_decayed, scores], axis=1), rows)
    k_i, k_j = iota((K, K), 0), iota((K, K), 1)
    ident = jnp.where(k_i == k_j, 1.0, 0.0).astype(F32)
    step = jnp.exp(closing) * ident - z[:, :K, K:]
    reach = jnp.exp(run) * query - z[:, K:, K:]
    carried = jnp.concatenate([z[0, :K, :K], step[0]], axis=1)
    r_ref[0:TB, :] = reach[0]
    o_ref[0:TB, :] = z[0, K:, :K]
    for b in range(1, nb):
        both = mm3(jnp.concatenate([step[b], reach[b]], axis=0), carried)
        o_ref[b * TB:(b + 1) * TB, :] = both[K:, :K] + z[b, K:, :K]
        r_ref[b * TB:(b + 1) * TB, :] = both[K:, K:]
        carried = both[:K] + jnp.concatenate([z[b, :K, :K], jnp.zeros((K, K), F32)], axis=1)
    sp_ref[0] = carried


def transitions(queries, keys, vals, beta_rates, log_gate):
    tokens, width = queries.shape
    heads = log_gate.shape[1]
    nb = tokens // TB
    whole = pl.BlockSpec(memory_space=pltpu.VMEM)
    head_rows = pl.BlockSpec((tokens, K), lambda h: (0, h))
    head_pair = pl.BlockSpec((2, tokens, K), lambda h: (0, 0, h))
    return pl.pallas_call(
        functools.partial(transition_kernel, nb),
        grid=(heads,),
        in_specs=[head_rows, head_pair, head_pair, whole, whole],
        out_specs=[pl.BlockSpec((1, K, 2 * K), lambda h: (h, 0, 0)), head_rows, head_rows],
        out_shape=[
            jax.ShapeDtypeStruct((heads, K, 2 * K), F32),
            jax.ShapeDtypeStruct((tokens, width), F32),
            jax.ShapeDtypeStruct((tokens, width), F32),
        ],
        scratch_shapes=[pltpu.VMEM((tokens, heads), F32), pltpu.VMEM((heads, nb * ROWS), F32)],
        compiler_params=pltpu.CompilerParams(vmem_limit_bytes=48 * 1024 * 1024),
        name="transitions",
    )(queries, keys, vals, beta_rates, log_gate)
MESH = pl.DeviceIdType.MESH


def place(wide_c):
    return jnp.concatenate([wide_c, jnp.zeros((K, K), F32)], axis=1)


def handoff_kernel(
    planes, sp_ref, in_ref, end_ref, gath, pre, from_low, from_high, out_buf,
    send_a, recv_a, send_up, recv_up, send_dn, recv_dn, send_c, recv_c,
):
    heads = sp_ref.shape[0]
    seq, me_head = lax.axis_index("seq"), lax.axis_index("head")
    z, i = seq // heads, lax.rem(seq, heads)
    up = (lax.rem(z + 1, planes) * heads + i, me_head)
    down = (lax.rem(z + planes - 1, planes) * heads + i, me_head)
    n_up, n_dn = from_low.shape[0], from_high.shape[0]

    def peer(offset):
        return lax.rem(i + offset, heads)

    barrier = pltpu.get_barrier_semaphore()
    for offset in range(1, heads):
        pl.semaphore_signal(barrier, inc=1, device_id=(z * heads + peer(offset), me_head), device_id_type=MESH)
    for where in (up, down):
        pl.semaphore_signal(barrier, inc=1, device_id=where, device_id_type=MESH)
    pl.semaphore_wait(barrier, heads + 1)

    own = pltpu.make_async_copy(sp_ref.at[i], gath.at[i], recv_a.at[i])
    own.start()
    first = []
    for offset in range(1, heads):
        other = peer(offset)
        copy = pltpu.make_async_remote_copy(
            src_ref=sp_ref.at[other], dst_ref=gath.at[i], send_sem=send_a.at[offset - 1],
            recv_sem=recv_a.at[i], device_id=(z * heads + other, me_head), device_id_type=MESH,
        )
        copy.start()
        first.append(copy)

    def arrived(src):
        pltpu.make_async_copy(gath.at[src], gath.at[src], recv_a.at[src]).wait()

    arrived(0)
    pre[1] = gath[0]

    def chain(src, _):
        arrived(src)
        later = gath[src]
        pre[src + 1] = mm3(later[:, K:], pre[src]) + place(later[:, :K])
        return 0

    lax.fori_loop(1, heads, chain, 0)

    def hop(src, dst, send, recv, where):
        copy = pltpu.make_async_remote_copy(
            src_ref=src, dst_ref=dst, send_sem=send, recv_sem=recv, device_id=where, device_id_type=MESH
        )
        copy.start()
        return copy

    total = pre.at[heads]
    ups, dns = [], []
    k_i, k_j = iota((K, 2 * K), 0), iota((K, 2 * K), 1)
    acc = jnp.where(k_i + K == k_j, 1.0, 0.0).astype(F32)
    state = jnp.zeros((K, K), F32)
    ups.append(hop(total, from_low.at[0], send_up.at[0], recv_up.at[0], up))
    dns.append(hop(total, from_high.at[0], send_dn.at[0], recv_dn.at[0], down))
    for s in range(1, n_up + 1):
        ups[s - 1].wait_recv()
        if s < n_up:
            ups.append(hop(from_low.at[s - 1], from_low.at[s], send_up.at[s], recv_up.at[s], up))
        if s <= n_dn:
            dns[s - 1].wait_recv()
            if s < n_dn:
                dns.append(hop(from_high.at[s - 1], from_high.at[s], send_dn.at[s], recv_dn.at[s], down))
        earlier = from_low[s - 1]
        if s == 1:
            joined = earlier
        else:
            joined = mm3(acc[:, K:], earlier) + place(acc[:, :K])
        acc = jnp.where(z >= s, joined, acc)
        if s <= n_dn:
            wrapped = from_high[s - 1]
            if s == 1:
                moved = wrapped[:, :K]
            else:
                moved = mm3(wrapped[:, K:], state) + wrapped[:, :K]
            state = jnp.where(z + s >= planes, moved, state)
    start = mm3(acc[:, K:], state) + acc[:, :K]
    start_parts = split(start)

    last = []
    for offset in range(1, heads):
        other = peer(offset)
        part = pre[lax.max(other, 1)]
        moved = mm3(part[:, K:], start_parts) + part[:, :K]
        out_buf[offset - 1] = jnp.where(other == 0, start, moved)
        copy = pltpu.make_async_remote_copy(
            src_ref=out_buf.at[offset - 1], dst_ref=in_ref.at[i], send_sem=send_c.at[offset - 1],
            recv_sem=recv_c.at[i], device_id=(z * heads + other, me_head), device_id_type=MESH,
        )
        copy.start()
        last.append(copy)
    part = pre[lax.max(i, 1)]
    in_ref[i] = jnp.where(i == 0, start, mm3(part[:, K:], start_parts) + part[:, :K])
    part = pre[heads]
    end_ref[...] = mm3(part[:, K:], start_parts) + part[:, :K]
    for offset in range(1, heads):
        other = peer(offset)
        pltpu.make_async_copy(in_ref.at[other], in_ref.at[other], recv_c.at[other]).wait()
    for copy in first + ups + dns + last:
        copy.wait_send()


def handoff(sp, planes):
    heads = sp.shape[0]
    n_up, n_dn = planes // 2, planes - 1 - planes // 2
    dma = pltpu.SemaphoreType.DMA
    whole = pl.BlockSpec(memory_space=pltpu.VMEM)
    return pl.pallas_call(
        functools.partial(handoff_kernel, planes),
        in_specs=[whole],
        out_specs=[whole, whole],
        out_shape=[jax.ShapeDtypeStruct((heads, K, K), F32), jax.ShapeDtypeStruct((K, K), F32)],
        scratch_shapes=[
            pltpu.VMEM((heads, K, 2 * K), F32),
            pltpu.VMEM((heads + 1, K, 2 * K), F32),
            pltpu.VMEM((n_up, K, 2 * K), F32),
            pltpu.VMEM((n_dn, K, 2 * K), F32),
            pltpu.VMEM((heads - 1, K, K), F32),
            dma((heads - 1,)), dma((heads,)), dma((n_up,)), dma((n_up,)), dma((n_dn,)), dma((n_dn,)),
            dma((heads - 1,)), dma((heads,)),
        ],
        compiler_params=pltpu.CompilerParams(
            collective_id=1, has_side_effects=True, vmem_limit_bytes=32 * 1024 * 1024
        ),
        name="handoff",
    )(sp)


def project_kernel(
    planes, r_ref, o_ref, in_ref, gain_ref, w_ref, end_ref, pick_ref, out_ref, states_ref,
    w_buf, normed, part, relay, landed, finals, chosen, taken,
    w_sem, send_sem, relay_sem, land_sem, share_send, share_recv, give_send, give_recv,
):
    chunks, depth, width = w_buf.shape
    half = width // 2
    tokens = r_ref.shape[0]
    ring = part.shape[2]
    rows = tokens // ring
    heads = in_ref.shape[0]
    seq, me = lax.axis_index("seq"), lax.axis_index("head")
    right, left = lax.rem(me + 1, ring), lax.rem(me + ring - 1, ring)
    far = lax.rem(me + 2, ring)
    z, i = seq // heads, lax.rem(seq, heads)
    at_end = z == planes - 1

    def load(c):
        return pltpu.make_async_copy(w_ref.at[:, pl.ds(c * width, width)], w_buf.at[c], w_sem.at[c])

    for c in range(chunks):
        load(c).start()
    barrier = pltpu.get_barrier_semaphore()
    for where in (left, right):
        pl.semaphore_signal(barrier, inc=1, device_id=(seq, where), device_id_type=MESH)

    @pl.when(z != planes - 1)
    def _():
        source = (planes - 1) * heads + i
        pl.semaphore_signal(barrier, inc=1, device_id=(source, me), device_id_type=MESH)

    @pl.when(at_end)
    def _():
        for offset in range(1, heads):
            other = z * heads + lax.rem(i + offset, heads)
            pl.semaphore_signal(barrier, inc=1, device_id=(other, me), device_id_type=MESH)

    def share(offset):
        other = lax.rem(i + offset, heads)
        return pltpu.make_async_remote_copy(
            src_ref=end_ref, dst_ref=finals.at[i], send_sem=share_send.at[offset - 1],
            recv_sem=share_recv.at[i], device_id=(z * heads + other, me), device_id_type=MESH,
        )

    def give(plane):
        return pltpu.make_async_remote_copy(
            src_ref=chosen.at[plane], dst_ref=taken, send_sem=give_send.at[plane],
            recv_sem=give_recv.at[0], device_id=(plane * heads + i, me), device_id_type=MESH,
        )

    gain = gain_ref[...]
    for h in range(heads):
        cols = slice(h * K, (h + 1) * K)
        attended = o_ref[:, cols] + mm3(r_ref[:, cols], in_ref[h])
        scale = lax.rsqrt(jnp.mean(attended * attended, axis=-1, keepdims=True) + 1e-6)
        normed[:, cols] = (attended * scale * gain).astype(BF16)

    @pl.when(at_end)
    def _():
        pl.semaphore_wait(barrier, 2 + heads - 1 + planes - 1)
        finals[i] = end_ref[...]
        for offset in range(1, heads):
            share(offset).start()

    @pl.when(z != planes - 1)
    def _():
        pl.semaphore_wait(barrier, 2)

    def push(src, dst, kind, c, recv, where):
        return pltpu.make_async_remote_copy(
            src_ref=src, dst_ref=dst, send_sem=send_sem.at[c, kind], recv_sem=recv,
            device_id=(seq, where), device_id_type=MESH,
        )

    def far_a(c):
        return push(part.at[c, 0, far], relay.at[c, 0], 0, c, relay_sem.at[c, 0], right)

    def far_b(c):
        return push(part.at[c, 1, far], relay.at[c, 1], 1, c, relay_sem.at[c, 1], left)

    def near_b(c):
        return push(part.at[c, 1, right], landed.at[c, 1], 2, c, land_sem.at[c, 1], right)

    def near_a(c):
        return push(part.at[c, 0, left], landed.at[c, 2], 3, c, land_sem.at[c, 2], left)

    def sum_a(c):
        return push(part.at[c, 0, right], landed.at[c, 0], 4, c, land_sem.at[c, 0], right)

    def sum_b(c):
        return push(part.at[c, 1, left], landed.at[c, 3], 5, c, land_sem.at[c, 3], left)

    def merge(c):
        far_a(c).wait_recv()
        part[c, 0, right] = part[c, 0, right] + relay[c, 0]
        sum_a(c).start()
        far_b(c).wait_recv()
        part[c, 1, left] = part[c, 1, left] + relay[c, 1]
        sum_b(c).start()

    def compute(c):
        load(c).wait()
        got = lax.dot_general(
            normed[...], w_buf[c], (((1,), (0,)), ((), ())), preferred_element_type=F32
        )
        part[c, 0] = got[:, :half].reshape(ring, rows, half)
        part[c, 1] = got[:, half:].reshape(ring, rows, half)
        far_a(c).start()
        far_b(c).start()
        near_b(c).start()
        near_a(c).start()

    compute(0)

    def lap(c, _):
        compute(c)
        merge(c - 1)
        return 0

    lax.fori_loop(1, chunks, lap, 0)
    merge(chunks - 1)

    @pl.when(at_end)
    def _():
        for offset in range(1, heads):
            other = lax.rem(i + offset, heads)
            pltpu.make_async_copy(finals.at[other], finals.at[other], share_recv.at[other]).wait()
        for plane in range(planes):
            total = finals[0] * pick_ref[plane, 0]
            for h in range(1, heads):
                total = total + finals[h] * pick_ref[plane, h]
            if plane < planes - 1:
                chosen[plane] = total
                give(plane).start()
            else:
                taken[...] = total

    def finish(c, _):
        for copy in (sum_a(c), near_b(c), near_a(c), sum_b(c)):
            copy.wait_recv()
        one = part[c, 0, me] + landed[c, 0] + landed[c, 2]
        two = part[c, 1, me] + landed[c, 1] + landed[c, 3]
        out_ref[:, pl.ds(pl.multiple_of(c * width, width), width)] = jnp.concatenate(
            [one, two], axis=1
        ).astype(out_ref.dtype)
        for copy in (far_a(c), far_b(c), near_b(c), near_a(c), sum_a(c), sum_b(c)):
            copy.wait_send()
        return 0

    lax.fori_loop(0, chunks, finish, 0)

    @pl.when(at_end)
    def _():
        for offset in range(1, heads):
            share(offset).wait_send()
        for plane in range(planes - 1):
            give(plane).wait_send()

    @pl.when(z != planes - 1)
    def _():
        give(0).wait_recv()

    for h in range(heads):
        states_ref[0, h] = taken[...] * pick_ref[planes, h]


def project(reach, base, incoming, gain, out_weight, closing, pick, ring, chunks=8):
    tokens = reach.shape[0]
    depth, columns = out_weight.shape
    width = columns // chunks
    rows, half = tokens // ring, width // 2
    planes, heads = pick.shape[0] - 1, pick.shape[1]
    dma = pltpu.SemaphoreType.DMA
    whole = pl.BlockSpec(memory_space=pltpu.VMEM)
    return pl.pallas_call(
        functools.partial(project_kernel, planes),
        in_specs=[
            whole, whole, whole, whole, pl.BlockSpec(memory_space=pl.ANY), whole,
            pl.BlockSpec(memory_space=pltpu.SMEM),
        ],
        out_specs=[whole, whole],
        out_shape=[
            jax.ShapeDtypeStruct((rows, columns), BF16),
            jax.ShapeDtypeStruct((1, heads, K, K), F32),
        ],
        scratch_shapes=[
            pltpu.VMEM((chunks, depth, width), BF16),
            pltpu.VMEM((tokens, depth), BF16),
            pltpu.VMEM((chunks, 2, ring, rows, half), F32),
            pltpu.VMEM((chunks, 2, rows, half), F32),
            pltpu.VMEM((chunks, 4, rows, half), F32),
            pltpu.VMEM((heads, K, K), F32),
            pltpu.VMEM((planes - 1, K, K), F32),
            pltpu.VMEM((K, K), F32),
            dma((chunks,)), dma((chunks, 6)), dma((chunks, 2)), dma((chunks, 4)),
            dma((heads - 1,)), dma((heads,)), dma((planes - 1,)), dma((1,)),
        ],
        compiler_params=pltpu.CompilerParams(
            collective_id=2, has_side_effects=True, vmem_limit_bytes=48 * 1024 * 1024
        ),
        name="project",
    )(reach, base, incoming, gain, out_weight, closing, pick)


def per_device(
    queries, key_vectors, values, beta_rates, log_gate, norm_gain, out_weight, decode_owner
):
    heads = log_gate.shape[1]
    planes = lax.axis_size("seq") // heads
    sp, reach, base = transitions(
        queries, key_vectors.transpose(1, 0, 2), values.transpose(1, 0, 2), beta_rates, log_gate
    )
    incoming, closing = handoff(sp, planes)
    position = lax.axis_index("seq")
    column = jnp.arange(planes) * heads + lax.rem(position, heads)
    targets = jnp.concatenate([column, position[None]])
    pick = jnp.any(decode_owner[None] == targets[:, None, None], axis=1).astype(F32)
    mixed, decode_states = project(
        reach, base, incoming, norm_gain.reshape(1, K), out_weight, closing, pick,
        lax.axis_size("head"),
    )
    return mixed, decode_states


def solution(mesh):
    in_specs = (
        P("seq", "head"), P("seq", None, "head"), P("seq", None, "head"), P("seq", "head"),
        P("seq", "head"), P(), P("head", None), P(None, "head"),
    )
    out_specs = (P(("seq", "head"), None), P("seq", "head", None, None))
    return jax.shard_map(
        per_device, mesh=mesh, in_specs=in_specs, out_specs=out_specs, check_vma=False
    )
```

time: 1050 us -> 130 us (0.12)
  waiting for transfers between devices: 493 us -> 0 us
  other arithmetic: 333 us -> 0.17 us
  matrix products: 183 us -> 0 us
  Pallas kernels: 0 us -> 118 us
  local copies, waits for them, and re-layouts: 25.7 us -> 8.74 us
  between operations: 14.1 us -> 0.72 us
    another operation x3 -> x0, other arithmetic: 317 us -> none  [the longest x2 316 us: prepare(): jax.scipy.linalg.solve_triangular(system, right_side, lower=True, unit_di...]
    all_gather x2 -> x0, waiting for transfers between devices: 278 us -> none  [carried_in(): pieces = jax.tree.map(lambda part: lax.all_gather(part, axis), value)]
    dot_general x87 -> x0, matrix products: 179 us -> none  [the longest x76 136 us: product(): jnp.einsum('ywc,ycp->ywp', left_factor, right_factor, precision=EXACT_PRE...]
    psum x1 -> x0, waiting for transfers between devices: 165 us -> none  [from_root(): return lax.psum(kept, axis)]
    pallas_call x0 -> x3, Pallas kernels: none -> 118 us  [the longest x1 48.5 us: handoff(): pl.pallas_call(functools.partial(handoff_kernel, planes), in_specs=[whole...]
    reduce_scatter x1 -> x0, waiting for transfers between devices: 49.3 us -> none  [per_device(): lax.psum_scatter(jnp.dot(normed, out_weight, preferred_element_type=jnp.f...]
  transfers between devices with their start and end apart: 4 -> 0, of which waited for: 4 -> 0; matrix products, arithmetic and copies ran while one was open for 2% -> 0% of each run, Pallas kernels for 0% -> 0%
where the time goes in v1:
time: 130 us; the launch traced here: 128 us
  Pallas kernels  118 us (91%)
  local copies, waits for them, and re-layouts  8.74 us (7%)
    pallas_call x1, Pallas kernels, handoff(): pl.pallas_call(functools.partial(handoff_kernel, planes), in_specs=[whole...  48.5 us
    pallas_call x1, Pallas kernels, project(): pl.pallas_call(functools.partial(project_kernel, planes), in_specs=[whole...  41.2 us
    pallas_call x1, Pallas kernels, transitions(): pl.pallas_call(functools.partial(transition_kernel, nb), grid=(heads,), i...  28.2 us
    unnamed x14, local copies, waits for them, and re-layouts  6.46 us

profile of v1, /device:TPU:1, one launch (start us, length us, event | category | flops | bytes accessed | tf_op | source)
XLA Modules:
  0.0 127.5 jit_solution(5320194156701772294)
XLA Ops:
  0.6 0.0 copy-start.3
  0.6 0.0 copy-start.4
  0.7 2.2 %copy_bitcast_fusion = (bf16[2,256,1024]{2,1,0:T(8,128)(2,1)S(1)}, bf16[2,256,1024]{2,1,0:T(8,128)(2,1)S(1)}) fusion(bf16[256,2,1024]{2,1,0:T(2,128)(2,1)} %param.10, bf16[256,2,1024]{2,1,0:T(2,128)(2,1)} %param.9), kind=kLoop, calls=%fused_computation | loop fusion | bytes 4194304 | tf_op jit(solution)/shard_map/transpose | solution.py:519
  2.8 0.8 copy.21.beta_ref
  3.7 0.8 copy.22.gate_ref
  4.5 0.0 copy-start.2
  4.5 1.0 copy-done.2
  5.5 28.2 %transitions.1 = (f32[8,128,256]{2,1,0:T(8,128)S(1)}, f32[256,1024]{1,0:T(8,128)S(1)}, f32[256,1024]{1,0:T(8,128)S(1)}) custom-call(bf16[256,1024]{1,0:T(8,128)(2,1)S(1)} %copy-done.2, bf16[2,256,1024]{2,1,0:T(8,128)(2,1)S(1)} %get-tuple-element.13.k_ref, bf16[2,256,1024]{2,1,0:T(8,128)(2,1)S(1)} %get-tuple-element.12.v_ref, f32[256,16]{1,0:T(8,128)S(1)} %copy.21.beta_ref, ...), custom_call_target="tpu_custom_call" | custom-call | tf_op jit(solution)/shard_map/transitions/pallas_call | solution.py:154
  33.7 0.0 copy-start
  33.7 1.0 copy-done
  34.7 48.5 %handoff.1 = (f32[8,128,128]{2,1,0:T(8,128)S(1)}, f32[128,128]{1,0:T(8,128)S(1)}) custom-call(f32[8,128,256]{2,1,0:T(8,128)S(1)} %get-tuple-element.9.sp_ref), custom_call_target="tpu_custom_call" | custom-call | tf_op jit(solution)/shard_map/handoff/pallas_call | solution.py:288
  83.2 0.1 pad_add_fusion
  83.3 0.0 copy-done.4
  83.3 0.1 compare_reduce_fusion
  83.4 0.1 copy.23.pick_ref
  83.5 0.0 copy-done.3
  83.5 0.0 copy-start.1
  83.5 1.2 copy-done.1
  84.7 41.2 %project.1 = (bf16[64,4096]{1,0:T(8,128)(2,1)S(1)}, f32[1,8,128,128]{3,2,1,0:T(8,128)S(1)}) custom-call(f32[256,1024]{1,0:T(8,128)S(1)} %get-tuple-element.7.r_ref, f32[256,1024]{1,0:T(8,128)S(1)} %copy-done.1, f32[8,128,128]{2,1,0:T(8,128)S(1)} %get-tuple-element.10.in_ref, f32[1,128]{1,0:T(1,128)S(1)} %bitcast.6, bf16[1024,4096]{1,0:T(8,128)(2,1)} %w_ref.1, ...), custom_call_target="tpu_custom_call" | custom-call | tf_op jit(solution)/shard_map/project/pallas_call | solution.py:483
  125.9 0.8 copy.28
  126.7 0.8 copy.29
  (2 shorter events, 0.0 us)
Async XLA Ops:
  0.6 82.9 %copy-start.3 = (f32[128]{0:T(128)S(1)}, f32[128]{0:T(128)}, u32[]{:S(2)}) copy-start(f32[128]{0:T(128)} %param.13) | copy-start | bytes 1540
  0.6 82.7 %copy-start.4 = (s32[2,8]{1,0:T(2,128)S(1)}, s32[2,8]{1,0:T(2,128)}, u32[]{:S(2)}) copy-start(s32[2,8]{1,0:T(2,128)} %param.15) | copy-start | bytes 196
  4.5 1.0 copy-start.2
  33.7 1.0 copy-start
  83.5 1.2 copy-start.1

commit v2 on v1

v2 whole, which is shorter than its diff:
```python
import functools
import jax
import jax.numpy as jnp
from jax import lax
from jax.experimental import pallas as pl
from jax.experimental.pallas import tpu as pltpu
from jax.sharding import PartitionSpec as P

K = 128
TB = 64
ROWS = 2 * TB
SUB = 8
F32 = jnp.float32
BF16 = jnp.bfloat16


def split(x):
    hi = x.astype(BF16)
    return hi, (x - hi.astype(F32)).astype(BF16)


def bdot(a, b):
    if a.ndim == 2:
        return lax.dot_general(a, b, (((1,), (0,)), ((), ())), preferred_element_type=F32)
    return lax.dot_general(a, b, (((2,), (1,)), ((0,), (0,))), preferred_element_type=F32)


def mm3(a, b):
    ah, al = a if isinstance(a, tuple) else split(a)
    bh, bl = b if isinstance(b, tuple) else split(b)
    wide = jnp.concatenate([ah, al], axis=-1)
    tall = jnp.concatenate([bh, bh], axis=-2)
    return bdot(wide, tall) + bdot(ah, bl)


def iota(shape, dim):
    return lax.broadcasted_iota(jnp.int32, shape, dim)


MESH = pl.DeviceIdType.MESH
PIECES = 2


def place(wide_c):
    return jnp.concatenate([wide_c, jnp.zeros(wide_c.shape, F32)], axis=-1)


def masks():
    r_i, s_i = iota((ROWS, ROWS), 0), iota((ROWS, ROWS), 1)
    return r_i, s_i, r_i % TB, s_i % TB


def decays(run, run_lane):
    seen = iota((TB, ROWS), 1) % TB <= iota((TB, ROWS), 0)
    return jnp.where(seen, jnp.exp(jnp.where(seen, run - run_lane, 0.0)), 0.0)


def invert(system, nb, r_t, s_t):
    near = (r_t // SUB) == (s_t // SUB)
    folded = jnp.sum(
        jnp.where(near, system, 0.0).reshape(nb, 2, TB // SUB, SUB, ROWS), axis=2
    ).reshape(nb * 2 * SUB, ROWS)
    e_i, e_l = iota((2 * SUB, ROWS), 0), iota((2 * SUB, ROWS), 1)
    eye = jnp.where(((e_i // SUB) == (e_l // TB)) & ((e_i % SUB) == (e_l % SUB)), 1.0, 0.0).astype(F32)
    inv = jnp.broadcast_to(eye, (nb, 2 * SUB, ROWS))
    base = (iota((nb * 2 * SUB, ROWS), 1) % TB) // SUB * SUB
    for i in range(SUB):
        for j in range(2):
            if i == SUB - 1 and j == 1:
                continue
            factor = jnp.take_along_axis(folded, base + (j * TB + i), axis=1, mode="promise_in_bounds")
            factor = factor.reshape(nb, 2 * SUB, ROWS)
            at = j * SUB + i
            inv = inv - factor * inv[:, at:at + 1, :]
    solve = jnp.broadcast_to(
        inv.reshape(nb, 2, 1, SUB, ROWS), (nb, 2, TB // SUB, SUB, ROWS)
    ).reshape(nb, ROWS, ROWS)
    solve = jnp.where(near, solve, 0.0)
    size = SUB
    while size < TB:
        pair = ((r_t // (2 * size)) == (s_t // (2 * size))) & ((r_t // size) > (s_t // size))
        parts = split(solve)
        solve = solve - mm3(parts, mm3(jnp.where(pair, system, 0.0), parts))
        size *= 2
    return solve


def whole_kernel(
    planes, q_ref, k_ref, v_ref, beta_ref, gate_ref, gain_ref, w_ref, pick_ref,
    out_ref, taken, q_buf, w_buf, run_scr, row_scr, beta_scr, sp, gath, rows_hi, rows_lo,
    kt_hi, kt_lo, carry, reach_scr, base_scr, from_low, from_high, out_buf, in_buf, end_buf,
    normed, part, relay, landed, finals, chosen,
    q_sem, w_sem, send_a, recv_a, send_up, recv_up, send_dn, recv_dn, send_c, recv_c,
    send_sem, relay_sem, land_sem, share_send, share_recv, give_send, give_recv,
):
    heads, tokens = gate_ref.shape
    nb = tokens // TB
    chunks, depth, width = w_buf.shape
    half = width // 2
    ring = part.shape[2]
    rows = tokens // ring
    seq, me = lax.axis_index("seq"), lax.axis_index("head")
    z, i = seq // heads, lax.rem(seq, heads)
    at_end = z == planes - 1
    up = (lax.rem(z + 1, planes) * heads + i, me)
    down = (lax.rem(z + planes - 1, planes) * heads + i, me)
    n_up, n_dn = from_low.shape[0], from_high.shape[0]
    right, left = lax.rem(me + 1, ring), lax.rem(me + ring - 1, ring)
    far = lax.rem(me + 2, ring)

    def peer(offset):
        return lax.rem(i + offset, heads)

    def load(c):
        return pltpu.make_async_copy(w_ref.at[:, pl.ds(c * width, width)], w_buf.at[c], w_sem.at[c])

    q_load = pltpu.make_async_copy(q_ref, q_buf, q_sem.at[0])
    q_load.start()
    for c in range(chunks):
        load(c).start()

    barrier = pltpu.get_barrier_semaphore()
    for offset in range(1, heads):
        pl.semaphore_signal(barrier, inc=1, device_id=(z * heads + peer(offset), me), device_id_type=MESH)
    for where in (up, down, (seq, right), (seq, left)):
        pl.semaphore_signal(barrier, inc=1, device_id=where, device_id_type=MESH)

    @pl.when(z != planes - 1)
    def _():
        source = (planes - 1) * heads + i
        pl.semaphore_signal(barrier, inc=1, device_id=(source, me), device_id_type=MESH)

    gate = gate_ref[...]
    t_i, s_i = iota((tokens, tokens), 0), iota((tokens, tokens), 1)
    upto = jnp.where(((t_i // TB) == (s_i // TB)) & (s_i <= t_i), 1.0, 0.0).astype(F32)
    run_scr[...] = lax.dot_general(
        upto, gate, (((1,), (1,)), ((), ())), precision=lax.Precision.HIGHEST, preferred_element_type=F32
    )
    t_j, l_j = iota((tokens, nb * ROWS), 0), iota((tokens, nb * ROWS), 1)
    spread = jnp.where(((t_j // TB) == (l_j // ROWS)) & ((t_j % TB) <= (l_j % TB)), 1.0, 0.0).astype(F32)
    row_scr[...] = lax.dot_general(
        gate, spread, (((1,), (0,)), ((), ())), precision=lax.Precision.HIGHEST, preferred_element_type=F32
    )
    same = jnp.where(t_i == s_i, 1.0, 0.0).astype(F32)
    beta_scr[...] = lax.dot_general(
        same, beta_ref[...], (((1,), (1,)), ((), ())), precision=lax.Precision.HIGHEST,
        preferred_element_type=F32,
    )

    def column(ref, h):
        lanes = iota(ref.shape, 1)
        return jnp.sum(jnp.where(lanes == h, ref[...], 0.0), axis=1, keepdims=True).reshape(nb, TB, 1)

    def lane_rows(h):
        picked = jnp.sum(
            jnp.where(iota((heads, nb * ROWS), 0) == h, row_scr[...], 0.0), axis=0, keepdims=True
        )
        return jnp.stack([picked[:, b * ROWS:(b + 1) * ROWS] for b in range(nb)], axis=0)

    def cols(h):
        return pl.ds(pl.multiple_of(h * K, K), K)

    def unit(x):
        x = x.astype(F32)
        return x * lax.rsqrt(jnp.sum(x * x, axis=-1, keepdims=True) + 1e-6)

    def give_a(h, step):
        return pltpu.make_async_remote_copy(
            src_ref=sp.at[h], dst_ref=gath.at[i], send_sem=send_a.at[step],
            recv_sem=recv_a.at[i], device_id=(z * heads + h, me), device_id_type=MESH,
        )

    def transition(step, _):
        h = lax.rem(i + 1 + step, heads)
        run = column(run_scr, h)
        run_lane = lane_rows(h)
        closing = run_lane[:, :, ROWS - 1:ROWS]
        rates = jnp.concatenate([column(beta_scr, 2 * h), column(beta_scr, 2 * h + 1)], axis=1)
        key = jnp.concatenate(
            [unit(k_ref[j, :, cols(h)]).reshape(nb, TB, K) for j in range(2)], axis=1
        )
        val = jnp.concatenate(
            [v_ref[j, :, cols(h)].astype(F32).reshape(nb, TB, K) for j in range(2)], axis=1
        )
        key_t = jnp.stack([key[b].T for b in range(nb)], axis=0)
        kth, ktl = split(key_t)
        kt_hi[h], kt_lo[h] = kth, ktl
        decay = decays(run, run_lane)
        r_i, s_i, r_t, s_t = masks()
        below = (r_t > s_t) | ((r_t == s_t) & (r_i > s_i))
        gram = mm3(key, (kth, ktl))
        system = jnp.where(below, rates * jnp.concatenate([decay, decay], axis=1) * gram, 0.0)
        solve = invert(system, nb, r_t, s_t)
        grown = jnp.exp(jnp.concatenate([run, run], axis=1))
        got = split(mm3(solve, jnp.concatenate([rates * val, (rates * grown) * key], axis=2)))
        rows_hi[h], rows_lo[h] = got
        z_rows = mm3(key_t * jnp.exp(closing - run_lane), got)
        k_i, k_j = iota((K, K), 0), iota((K, K), 1)
        ident = jnp.where(k_i == k_j, 1.0, 0.0).astype(F32)
        move = jnp.exp(closing) * ident - z_rows[:, :, K:]
        state = jnp.concatenate([z_rows[0, :, :K], move[0]], axis=1)
        for b in range(1, nb):
            carry[h, b - 1] = state
            state = mm3(move[b], state) + place(z_rows[b, :, :K])
        sp[h] = state

        @pl.when((step == 0) & at_end)
        def _():
            pl.semaphore_wait(barrier, heads + 3 + planes - 1)

        @pl.when((step == 0) & (z != planes - 1))
        def _():
            pl.semaphore_wait(barrier, heads + 3)

        @pl.when(step < heads - 1)
        def _():
            give_a(h, step).start()

        @pl.when(step == heads - 1)
        def _():
            gath[h] = state

        return 0

    lax.fori_loop(0, heads, transition, 0)

    def reaches(h, _):
        run = column(run_scr, h)
        query = q_buf[:, cols(h)].astype(F32).reshape(nb, TB, K)
        scores = mm3(query, (kt_hi[h], kt_lo[h])) * decays(run, lane_rows(h))
        z_out = mm3(scores, (rows_hi[h], rows_lo[h]))
        reach = jnp.exp(run) * query - z_out[:, :, K:]
        base_scr[0:TB, cols(h)] = z_out[0, :, :K]
        reach_scr[0:TB, cols(h)] = reach[0]
        both = mm3(reach[1:], carry[h])
        base_scr[TB:, cols(h)] = (both[:, :, :K] + z_out[1:, :, :K]).reshape(tokens - TB, K)
        reach_scr[TB:, cols(h)] = both[:, :, K:].reshape(tokens - TB, K)
        return 0

    for src in range(heads):
        @pl.when(src != i)
        def _():
            pltpu.make_async_copy(gath.at[src], gath.at[src], recv_a.at[src]).wait()
    size = 1
    while size < heads:
        for begin in range(0, heads, 2 * size):
            lo, hi = begin + size, begin + 2 * size
            later = gath[lo:hi]
            joined = mm3(later[:, :, K:].reshape(size * K, K), gath[lo - 1]).reshape(size, K, 2 * K)
            gath[lo:hi] = joined + place(later[:, :, :K])
        size *= 2

    bit = K // PIECES

    def hop(s, p, upward):
        slots = from_low if upward else from_high
        src = gath.at[heads - 1] if s == 0 else slots.at[s - 1]
        send, recv = (send_up, recv_up) if upward else (send_dn, recv_dn)
        lines = pl.ds(p * bit, bit)
        return pltpu.make_async_remote_copy(
            src_ref=src.at[lines], dst_ref=slots.at[s, lines], send_sem=send.at[s, p],
            recv_sem=recv.at[s, p], device_id=up if upward else down, device_id_type=MESH,
        )

    for p in range(PIECES):
        hop(0, p, True).start()
        hop(0, p, False).start()
    q_load.wait()
    k_i, k_j = iota((K, 2 * K), 0), iota((K, 2 * K), 1)
    acc = jnp.where(k_i + K == k_j, 1.0, 0.0).astype(F32)
    state = jnp.zeros((K, K), F32)
    each = heads // n_up
    for s in range(n_up):
        lax.fori_loop(s * each, (s + 1) * each, reaches, 0)
        for p in range(PIECES):
            hop(s, p, True).wait_recv()
            if s + 1 < n_up:
                hop(s + 1, p, True).start()
            if s < n_dn:
                hop(s, p, False).wait_recv()
                if s + 1 < n_dn:
                    hop(s + 1, p, False).start()
        earlier = from_low[s]
        joined = earlier if s == 0 else mm3(acc[:, K:], earlier) + place(acc[:, :K])
        acc = jnp.where(z >= s + 1, joined, acc)
        if s < n_dn:
            wrapped = from_high[s]
            moved = wrapped[:, :K] if s == 0 else mm3(wrapped[:, K:], state) + wrapped[:, :K]
            state = jnp.where(z + s + 1 >= planes, moved, state)
    start = mm3(acc[:, K:], state) + acc[:, :K]

    prefix = gath[...]
    spread_out = mm3(prefix[:, :, K:].reshape(heads * K, K), start).reshape(heads, K, K) + prefix[:, :, :K]
    out_buf[0] = start
    out_buf[1:] = spread_out[:heads - 1]
    end_buf[...] = spread_out[heads - 1]

    def give_c(offset):
        other = peer(offset)
        return pltpu.make_async_remote_copy(
            src_ref=out_buf.at[other], dst_ref=in_buf.at[i], send_sem=send_c.at[offset - 1],
            recv_sem=recv_c.at[i], device_id=(z * heads + other, me), device_id_type=MESH,
        )

    def share(offset):
        other = peer(offset)
        return pltpu.make_async_remote_copy(
            src_ref=end_buf, dst_ref=finals.at[i], send_sem=share_send.at[offset - 1],
            recv_sem=share_recv.at[i], device_id=(z * heads + other, me), device_id_type=MESH,
        )

    def give(plane):
        return pltpu.make_async_remote_copy(
            src_ref=chosen.at[plane], dst_ref=taken, send_sem=give_send.at[plane],
            recv_sem=give_recv.at[0], device_id=(plane * heads + i, me), device_id_type=MESH,
        )

    for offset in range(1, heads):
        give_c(offset).start()
    in_buf[i] = out_buf[i]

    @pl.when(at_end)
    def _():
        finals[i] = end_buf[...]
        for offset in range(1, heads):
            share(offset).start()

    gain = gain_ref[...]

    def attend(offset, _):
        h = peer(offset)

        @pl.when(offset > 0)
        def _():
            pltpu.make_async_copy(in_buf.at[h], in_buf.at[h], recv_c.at[h]).wait()

        attended = base_scr[:, cols(h)] + mm3(reach_scr[:, cols(h)], in_buf[h])
        scale = lax.rsqrt(jnp.mean(attended * attended, axis=-1, keepdims=True) + 1e-6)
        normed[:, cols(h)] = (attended * scale * gain).astype(BF16)
        return 0

    lax.fori_loop(0, heads, attend, 0)

    def push(src, dst, kind, c, recv, where):
        return pltpu.make_async_remote_copy(
            src_ref=src, dst_ref=dst, send_sem=send_sem.at[c, kind], recv_sem=recv,
            device_id=(seq, where), device_id_type=MESH,
        )

    def far_a(c):
        return push(part.at[c, 0, far], relay.at[c, 0], 0, c, relay_sem.at[c, 0], right)

    def far_b(c):
        return push(part.at[c, 1, far], relay.at[c, 1], 1, c, relay_sem.at[c, 1], left)

    def near_b(c):
        return push(part.at[c, 1, right], landed.at[c, 1], 2, c, land_sem.at[c, 1], right)

    def near_a(c):
        return push(part.at[c, 0, left], landed.at[c, 2], 3, c, land_sem.at[c, 2], left)

    def sum_a(c):
        return push(part.at[c, 0, right], landed.at[c, 0], 4, c, land_sem.at[c, 0], right)

    def sum_b(c):
        return push(part.at[c, 1, left], landed.at[c, 3], 5, c, land_sem.at[c, 3], left)

    def merge(c):
        far_a(c).wait_recv()
        part[c, 0, right] = part[c, 0, right] + relay[c, 0]
        sum_a(c).start()
        far_b(c).wait_recv()
        part[c, 1, left] = part[c, 1, left] + relay[c, 1]
        sum_b(c).start()

    def compute(c):
        load(c).wait()
        got = lax.dot_general(
            normed[...], w_buf[c], (((1,), (0,)), ((), ())), preferred_element_type=F32
        )
        part[c, 0] = got[:, :half].reshape(ring, rows, half)
        part[c, 1] = got[:, half:].reshape(ring, rows, half)
        far_a(c).start()
        far_b(c).start()
        near_b(c).start()
        near_a(c).start()

    compute(0)

    def lap(c, _):
        compute(c)
        merge(c - 1)
        return 0

    lax.fori_loop(1, chunks, lap, 0)
    merge(chunks - 1)

    @pl.when(at_end)
    def _():
        for offset in range(1, heads):
            other = lax.rem(i + offset, heads)
            pltpu.make_async_copy(finals.at[other], finals.at[other], share_recv.at[other]).wait()
        for plane in range(planes):
            total = finals[0] * pick_ref[plane, 0]
            for h in range(1, heads):
                total = total + finals[h] * pick_ref[plane, h]
            if plane < planes - 1:
                chosen[plane] = total
                give(plane).start()
            else:
                taken[...] = total

    def finish(c, _):
        for copy in (sum_a(c), near_b(c), near_a(c), sum_b(c)):
            copy.wait_recv()
        one = part[c, 0, me] + landed[c, 0] + landed[c, 2]
        two = part[c, 1, me] + landed[c, 1] + landed[c, 3]
        out_ref[:, pl.ds(pl.multiple_of(c * width, width), width)] = jnp.concatenate(
            [one, two], axis=1
        ).astype(out_ref.dtype)
        for copy in (far_a(c), far_b(c), near_b(c), near_a(c), sum_a(c), sum_b(c)):
            copy.wait_send()
        return 0

    lax.fori_loop(0, chunks, finish, 0)

    @pl.when(at_end)
    def _():
        for offset in range(1, heads):
            share(offset).wait_send()
        for plane in range(planes - 1):
            give(plane).wait_send()

    @pl.when(z != planes - 1)
    def _():
        give(0).wait_recv()

    for step in range(heads - 1):
        give_a(lax.rem(i + 1 + step, heads), step).wait_send()
        give_c(step + 1).wait_send()
    for p in range(PIECES):
        for s in range(n_up):
            hop(s, p, True).wait_send()
        for s in range(n_dn):
            hop(s, p, False).wait_send()


def whole(queries, keys, vals, beta_rates, log_gate, gain, out_weight, pick, ring, chunks=8):
    tokens, wide = queries.shape
    planes, heads = pick.shape
    nb = tokens // TB
    depth, columns = out_weight.shape
    width = columns // chunks
    rows, half = tokens // ring, width // 2
    n_up, n_dn = planes // 2, planes - 1 - planes // 2
    dma = pltpu.SemaphoreType.DMA
    vmem = pl.BlockSpec(memory_space=pltpu.VMEM)
    outside = pl.BlockSpec(memory_space=pl.ANY)
    pair = (heads, K, 2 * K)
    return pl.pallas_call(
        functools.partial(whole_kernel, planes),
        in_specs=[outside, vmem, vmem, vmem, vmem, vmem, outside, pl.BlockSpec(memory_space=pltpu.SMEM)],
        out_specs=[vmem, vmem],
        out_shape=[jax.ShapeDtypeStruct((rows, columns), BF16), jax.ShapeDtypeStruct((K, K), F32)],
        scratch_shapes=[
            pltpu.VMEM((tokens, wide), BF16),
            pltpu.VMEM((chunks, depth, width), BF16),
            pltpu.VMEM((tokens, heads), F32),
            pltpu.VMEM((heads, nb * ROWS), F32),
            pltpu.VMEM((tokens, 2 * heads), F32),
            pltpu.VMEM(pair, F32),
            pltpu.VMEM(pair, F32),
            pltpu.VMEM((heads, nb, ROWS, 2 * K), BF16),
            pltpu.VMEM((heads, nb, ROWS, 2 * K), BF16),
            pltpu.VMEM((heads, nb, K, ROWS), BF16),
            pltpu.VMEM((heads, nb, K, ROWS), BF16),
            pltpu.VMEM((heads, nb - 1, K, 2 * K), F32),
            pltpu.VMEM((tokens, wide), F32),
            pltpu.VMEM((tokens, wide), F32),
            pltpu.VMEM((n_up, K, 2 * K), F32),
            pltpu.VMEM((n_dn, K, 2 * K), F32),
            pltpu.VMEM((heads, K, K), F32),
            pltpu.VMEM((heads, K, K), F32),
            pltpu.VMEM((K, K), F32),
            pltpu.VMEM((tokens, depth), BF16),
            pltpu.VMEM((chunks, 2, ring, rows, half), F32),
            pltpu.VMEM((chunks, 2, rows, half), F32),
            pltpu.VMEM((chunks, 4, rows, half), F32),
            pltpu.VMEM((heads, K, K), F32),
            pltpu.VMEM((planes - 1, K, K), F32),
            dma((1,)), dma((chunks,)), dma((heads - 1,)), dma((heads,)),
            dma((n_up, PIECES)), dma((n_up, PIECES)), dma((n_dn, PIECES)), dma((n_dn, PIECES)),
            dma((heads - 1,)), dma((heads,)),
            dma((chunks, 6)), dma((chunks, 2)), dma((chunks, 4)),
            dma((heads - 1,)), dma((heads,)), dma((planes - 1,)), dma((1,)),
        ],
        compiler_params=pltpu.CompilerParams(
            collective_id=1, has_side_effects=True, vmem_limit_bytes=50 * 1024 * 1024
        ),
        name="whole",
    )(queries, keys, vals, beta_rates, log_gate, gain, out_weight, pick)


def per_device(
    queries, key_vectors, values, beta_rates, log_gate, norm_gain, out_weight, decode_owner
):
    heads = log_gate.shape[1]
    planes = lax.axis_size("seq") // heads
    position = lax.axis_index("seq")
    column = jnp.arange(planes) * heads + lax.rem(position, heads)
    pick = jnp.any(decode_owner[None] == column[:, None, None], axis=1).astype(F32)
    mixed, taken = whole(
        queries, key_vectors.transpose(1, 0, 2), values.transpose(1, 0, 2), beta_rates.T, log_gate.T,
        norm_gain.reshape(1, K), out_weight, pick, lax.axis_size("head"),
    )
    owned = jnp.any(decode_owner == position, axis=0)
    decode_states = jnp.where(owned[:, None, None], taken[None], 0.0)[None]
    return mixed, decode_states


def solution(mesh):
    in_specs = (
        P("seq", "head"), P("seq", None, "head"), P("seq", None, "head"), P("seq", "head"),
        P("seq", "head"), P(), P("head", None), P(None, "head"),
    )
    out_specs = (P(("seq", "head"), None), P("seq", "head", None, None))
    return jax.shard_map(
        per_device, mesh=mesh, in_specs=in_specs, out_specs=out_specs, check_vma=False
    )
```

time: 130 us -> 110 us (0.85); the launches traced: 128 us -> 109 us
  Pallas kernels: 118 us -> 100 us
  local copies, waits for them, and re-layouts: 8.74 us -> 6.07 us
  other arithmetic: 0.17 us -> 2.37 us
    pallas_call x3 -> x1, Pallas kernels: 118 us -> 100 us  [whole(): pl.pallas_call(functools.partial(whole_kernel, planes), in_specs=[outside...]
    unnamed x14 -> x9, local copies, waits for them, and re-layouts: 6.46 us -> 3.9 us
    reduce_or x1 -> x2, other arithmetic: 0.08 us -> 1.46 us  [the longest x1 0.75 us: per_device(): jnp.any(decode_owner[None] == column[:, None, None], axis=1).astype(F32)]
where the time goes in v2:
time: 110 us; the launch traced here: 109 us
  Pallas kernels  100 us (91%)
  local copies, waits for them, and re-layouts  6.07 us (6%)
  other arithmetic  2.37 us (2%)
    pallas_call x1, Pallas kernels, whole(): pl.pallas_call(functools.partial(whole_kernel, planes), in_specs=[outside...  100 us
    unnamed x9, local copies, waits for them, and re-layouts  3.9 us

profile of v2, /device:TPU:1, one launch (start us, length us, event | category | flops | bytes accessed | tf_op | source)
XLA Modules:
  0.0 109.3 jit_solution(10386338614923027252)
XLA Ops:
  0.6 0.7 compare_reduce_fusion.1
  1.3 0.8 compare_reduce_fusion
  2.1 2.2 %copy_bitcast_fusion = (bf16[2,256,1024]{2,1,0:T(8,128)(2,1)S(1)}, bf16[2,256,1024]{2,1,0:T(8,128)(2,1)S(1)}) fusion(bf16[256,2,1024]{2,1,0:T(2,128)(2,1)} %param.10, bf16[256,2,1024]{2,1,0:T(2,128)(2,1)} %param.9), kind=kLoop, calls=%fused_computation | loop fusion | bytes 4194304 | tf_op jit(solution)/shard_map/transpose | solution.py:513
  4.3 0.0 copy-start
  4.3 1.0 copy-done
  5.3 0.0 copy-start.1
  5.3 0.7 copy-done.1
  6.0 0.0 copy-start.2
  6.0 0.7 copy-done.2
  6.7 0.0 copy-start.3
  6.7 0.7 copy-done.3
  7.4 100.2 %whole.1 = (bf16[64,4096]{1,0:T(8,128)(2,1)S(1)}, f32[128,128]{1,0:T(8,128)S(1)}) custom-call(bf16[256,1024]{1,0:T(8,128)(2,1)S(1)} %copy-done, bf16[2,256,1024]{2,1,0:T(8,128)(2,1)S(1)} %get-tuple-element.7.k_ref, bf16[2,256,1024]{2,1,0:T(8,128)(2,1)S(1)} %get-tuple-element.6.v_ref, f32[16,256]{1,0:T(8,128)S(1)} %bitcast.7, f32[8,256]{1,0:T(8,128)S(1)} %bitcast.8, ...), custom_call_target="tpu_custom_call" | custom-call | tf_op jit(solution)/shard_map/whole/pallas_call | solution.py:460
  107.6 0.9 broadcast_select_fusion
  108.5 0.8 copy.17
  (2 shorter events, 0.0 us)
Async XLA Ops:
  4.3 1.0 copy-start
  5.3 0.7 copy-start.1
  6.0 0.7 copy-start.2
  6.7 0.7 copy-start.3

commit v3 on v2

--- a/solution.py
+++ b/solution.py
@@ -39,6 +39,7 @@
 
 MESH = pl.DeviceIdType.MESH
 PIECES = 2
+GROUP = 2
 
 
 def place(wide_c):
@@ -86,11 +87,11 @@
 
 
 def whole_kernel(
-    planes, q_ref, k_ref, v_ref, beta_ref, gate_ref, gain_ref, w_ref, pick_ref,
-    out_ref, taken, q_buf, w_buf, run_scr, row_scr, beta_scr, sp, gath, rows_hi, rows_lo,
+    planes, q_ref, k_hbm, v_hbm, beta_hbm, gate_hbm, gain_hbm, w_ref, owner_hbm,
+    out_ref, states_ref, taken, owner_ref, gain_ref, beta_ref, gate_ref, k_ref, v_ref, q_buf, w_buf, run_scr, row_scr, beta_scr, sp, gath, rows_hi, rows_lo,
     kt_hi, kt_lo, carry, reach_scr, base_scr, from_low, from_high, out_buf, in_buf, end_buf,
     normed, part, relay, landed, finals, chosen,
-    q_sem, w_sem, send_a, recv_a, send_up, recv_up, send_dn, recv_dn, send_c, recv_c,
+    q_sem, in_sem, k_sem, w_sem, send_a, recv_a, send_up, recv_up, send_dn, recv_dn, send_c, recv_c,
     send_sem, relay_sem, land_sem, share_send, share_recv, give_send, give_recv,
 ):
     heads, tokens = gate_ref.shape
@@ -115,6 +116,29 @@
         return pltpu.make_async_copy(w_ref.at[:, pl.ds(c * width, width)], w_buf.at[c], w_sem.at[c])
 
     q_load = pltpu.make_async_copy(q_ref, q_buf, q_sem.at[0])
+    small = [
+        pltpu.make_async_copy(src, dst, in_sem.at[n])
+        for n, (src, dst) in enumerate(
+            [(gate_hbm, gate_ref), (beta_hbm, beta_ref), (gain_hbm, gain_ref), (owner_hbm, owner_ref)]
+        )
+    ]
+    pairs = heads // GROUP
+
+    def load_pair(n):
+        pair = lax.rem(i // GROUP + 1 + n, pairs)
+        lanes = pl.ds(pl.multiple_of(pair * GROUP * K, GROUP * K), GROUP * K)
+        return [
+            pltpu.make_async_copy(src.at[:, :, lanes], dst.at[pair], k_sem.at[n, j])
+            for j, (src, dst) in enumerate([(k_hbm, k_ref), (v_hbm, v_ref)])
+        ]
+
+    for copy in small[:2]:
+        copy.start()
+    for n in range(pairs):
+        for copy in load_pair(n):
+            copy.start()
+    for copy in small[2:]:
+        copy.start()
     q_load.start()
     for c in range(chunks):
         load(c).start()
@@ -130,6 +154,8 @@
         source = (planes - 1) * heads + i
         pl.semaphore_signal(barrier, inc=1, device_id=(source, me), device_id_type=MESH)
 
+    for copy in small:
+        copy.wait()
     gate = gate_ref[...]
     t_i, s_i = iota((tokens, tokens), 0), iota((tokens, tokens), 1)
     upto = jnp.where(((t_i // TB) == (s_i // TB)) & (s_i <= t_i), 1.0, 0.0).astype(F32)
@@ -147,62 +173,77 @@
         preferred_element_type=F32,
     )
 
-    def column(ref, h):
+    batch = GROUP * nb
+
+    def column(ref, lanes_at):
         lanes = iota(ref.shape, 1)
-        return jnp.sum(jnp.where(lanes == h, ref[...], 0.0), axis=1, keepdims=True).reshape(nb, TB, 1)
-
-    def lane_rows(h):
-        picked = jnp.sum(
-            jnp.where(iota((heads, nb * ROWS), 0) == h, row_scr[...], 0.0), axis=0, keepdims=True
-        )
-        return jnp.stack([picked[:, b * ROWS:(b + 1) * ROWS] for b in range(nb)], axis=0)
-
-    def cols(h):
-        return pl.ds(pl.multiple_of(h * K, K), K)
+        got = [
+            jnp.sum(jnp.where(lanes == at, ref[...], 0.0), axis=1, keepdims=True).reshape(nb, TB, 1)
+            for at in lanes_at
+        ]
+        return jnp.concatenate(got, axis=0)
+
+    def lane_rows(h0):
+        got = []
+        for g in range(GROUP):
+            picked = jnp.sum(
+                jnp.where(iota((heads, nb * ROWS), 0) == h0 + g, row_scr[...], 0.0), axis=0, keepdims=True
+            )
+            got += [picked[:, b * ROWS:(b + 1) * ROWS] for b in range(nb)]
+        return jnp.stack(got, axis=0)
+
+    def group_cols(h0):
+        return pl.ds(pl.multiple_of(h0 * K, GROUP * K), GROUP * K)
+
+    def by_head(x):
+        return jnp.concatenate([x[:, g * K:(g + 1) * K].reshape(nb, TB, K) for g in range(GROUP)], axis=0)
 
     def unit(x):
-        x = x.astype(F32)
         return x * lax.rsqrt(jnp.sum(x * x, axis=-1, keepdims=True) + 1e-6)
 
-    def give_a(h, step):
+    def give_a(h):
+        where = jnp.where(h > i, h - 1, h)
         return pltpu.make_async_remote_copy(
-            src_ref=sp.at[h], dst_ref=gath.at[i], send_sem=send_a.at[step],
+            src_ref=sp.at[h], dst_ref=gath.at[i], send_sem=send_a.at[where],
             recv_sem=recv_a.at[i], device_id=(z * heads + h, me), device_id_type=MESH,
         )
 
     def transition(step, _):
-        h = lax.rem(i + 1 + step, heads)
-        run = column(run_scr, h)
-        run_lane = lane_rows(h)
+        pair = lax.rem(i // GROUP + 1 + step, pairs)
+        h0 = pair * GROUP
+        for src, j in ((k_hbm, 0), (v_hbm, 1)):
+            dst = (k_ref, v_ref)[j]
+            pltpu.make_async_copy(dst.at[pair], dst.at[pair], k_sem.at[step, j]).wait()
+        run = column(run_scr, [h0 + g for g in range(GROUP)])
+        run_lane = lane_rows(h0)
         closing = run_lane[:, :, ROWS - 1:ROWS]
-        rates = jnp.concatenate([column(beta_scr, 2 * h), column(beta_scr, 2 * h + 1)], axis=1)
-        key = jnp.concatenate(
-            [unit(k_ref[j, :, cols(h)]).reshape(nb, TB, K) for j in range(2)], axis=1
-        )
-        val = jnp.concatenate(
-            [v_ref[j, :, cols(h)].astype(F32).reshape(nb, TB, K) for j in range(2)], axis=1
-        )
-        key_t = jnp.stack([key[b].T for b in range(nb)], axis=0)
+        rates = jnp.concatenate(
+            [column(beta_scr, [2 * (h0 + g) + j for g in range(GROUP)]) for j in range(2)], axis=1
+        )
+        key = unit(jnp.concatenate([by_head(k_ref[pair, j].astype(F32)) for j in range(2)], axis=1))
+        val = jnp.concatenate([by_head(v_ref[pair, j].astype(F32)) for j in range(2)], axis=1)
+        key_t = jnp.stack([key[b].T for b in range(batch)], axis=0)
         kth, ktl = split(key_t)
-        kt_hi[h], kt_lo[h] = kth, ktl
+        kt_hi[pair], kt_lo[pair] = kth, ktl
         decay = decays(run, run_lane)
         r_i, s_i, r_t, s_t = masks()
         below = (r_t > s_t) | ((r_t == s_t) & (r_i > s_i))
         gram = mm3(key, (kth, ktl))
         system = jnp.where(below, rates * jnp.concatenate([decay, decay], axis=1) * gram, 0.0)
-        solve = invert(system, nb, r_t, s_t)
+        solve = invert(system, batch, r_t, s_t)
         grown = jnp.exp(jnp.concatenate([run, run], axis=1))
         got = split(mm3(solve, jnp.concatenate([rates * val, (rates * grown) * key], axis=2)))
-        rows_hi[h], rows_lo[h] = got
+        rows_hi[pair], rows_lo[pair] = got
         z_rows = mm3(key_t * jnp.exp(closing - run_lane), got)
         k_i, k_j = iota((K, K), 0), iota((K, K), 1)
         ident = jnp.where(k_i == k_j, 1.0, 0.0).astype(F32)
-        move = jnp.exp(closing) * ident - z_rows[:, :, K:]
-        state = jnp.concatenate([z_rows[0, :, :K], move[0]], axis=1)
+        move = (jnp.exp(closing) * ident - z_rows[:, :, K:]).reshape(GROUP, nb, K, K)
+        fresh = z_rows[:, :, :K].reshape(GROUP, nb, K, K)
+        state = jnp.concatenate([fresh[:, 0], move[:, 0]], axis=2)
         for b in range(1, nb):
-            carry[h, b - 1] = state
-            state = mm3(move[b], state) + place(z_rows[b, :, :K])
-        sp[h] = state
+            carry[pair, b - 1] = state
+            state = mm3(move[:, b], state) + place(fresh[:, b])
+        sp[pl.ds(h0, GROUP)] = state
 
         @pl.when((step == 0) & at_end)
         def _():
@@ -212,29 +253,34 @@
         def _():
             pl.semaphore_wait(barrier, heads + 3)
 
-        @pl.when(step < heads - 1)
-        def _():
-            give_a(h, step).start()
-
-        @pl.when(step == heads - 1)
-        def _():
-            gath[h] = state
-
-        return 0
-
-    lax.fori_loop(0, heads, transition, 0)
-
-    def reaches(h, _):
-        run = column(run_scr, h)
-        query = q_buf[:, cols(h)].astype(F32).reshape(nb, TB, K)
-        scores = mm3(query, (kt_hi[h], kt_lo[h])) * decays(run, lane_rows(h))
-        z_out = mm3(scores, (rows_hi[h], rows_lo[h]))
-        reach = jnp.exp(run) * query - z_out[:, :, K:]
-        base_scr[0:TB, cols(h)] = z_out[0, :, :K]
-        reach_scr[0:TB, cols(h)] = reach[0]
-        both = mm3(reach[1:], carry[h])
-        base_scr[TB:, cols(h)] = (both[:, :, :K] + z_out[1:, :, :K]).reshape(tokens - TB, K)
-        reach_scr[TB:, cols(h)] = both[:, :, K:].reshape(tokens - TB, K)
+        for g in range(GROUP):
+            @pl.when(h0 + g != i)
+            def _():
+                give_a(h0 + g).start()
+
+            @pl.when(h0 + g == i)
+            def _():
+                gath[i] = state[g]
+
+        return 0
+
+    lax.fori_loop(0, pairs, transition, 0)
+
+    def reaches(pair, _):
+        h0 = pair * GROUP
+        run = column(run_scr, [h0 + g for g in range(GROUP)])
+        query = by_head(q_buf[:, group_cols(h0)].astype(F32))
+        scores = mm3(query, (kt_hi[pair], kt_lo[pair])) * decays(run, lane_rows(h0))
+        z_out = mm3(scores, (rows_hi[pair], rows_lo[pair])).reshape(GROUP, nb, TB, 2 * K)
+        reach = (jnp.exp(run) * query).reshape(GROUP, nb, TB, K) - z_out[..., K:]
+        base = [z_out[:, 0, :, :K]]
+        whole_reach = [reach[:, 0]]
+        for b in range(1, nb):
+            both = mm3(reach[:, b], carry[pair, b - 1])
+            base.append(both[:, :, :K] + z_out[:, b, :, :K])
+            whole_reach.append(both[:, :, K:])
+        base_scr[pl.ds(h0, GROUP)] = jnp.concatenate(base, axis=1)
+        reach_scr[pl.ds(h0, GROUP)] = jnp.concatenate(whole_reach, axis=1)
         return 0
 
     for src in range(heads):
@@ -269,7 +315,7 @@
     k_i, k_j = iota((K, 2 * K), 0), iota((K, 2 * K), 1)
     acc = jnp.where(k_i + K == k_j, 1.0, 0.0).astype(F32)
     state = jnp.zeros((K, K), F32)
-    each = heads // n_up
+    each = pairs // n_up
     for s in range(n_up):
         lax.fori_loop(s * each, (s + 1) * each, reaches, 0)
         for p in range(PIECES):
@@ -327,19 +373,27 @@
 
     gain = gain_ref[...]
 
-    def attend(offset, _):
-        h = peer(offset)
-
-        @pl.when(offset > 0)
-        def _():
-            pltpu.make_async_copy(in_buf.at[h], in_buf.at[h], recv_c.at[h]).wait()
-
-        attended = base_scr[:, cols(h)] + mm3(reach_scr[:, cols(h)], in_buf[h])
+    def owned(device):
+        found = jnp.where(owner_ref[...] == device, 1.0, 0.0).astype(F32)
+        return jnp.max(found, axis=0, keepdims=True)
+
+
+    def attend(step, _):
+        pair = lax.rem(i // GROUP + step, pairs)
+        h0 = pair * GROUP
+        for g in range(GROUP):
+            @pl.when(h0 + g != i)
+            def _():
+                pltpu.make_async_copy(in_buf.at[h0 + g], in_buf.at[h0 + g], recv_c.at[h0 + g]).wait()
+
+        these = pl.ds(h0, GROUP)
+        attended = base_scr[these] + mm3(reach_scr[these], in_buf[these])
         scale = lax.rsqrt(jnp.mean(attended * attended, axis=-1, keepdims=True) + 1e-6)
-        normed[:, cols(h)] = (attended * scale * gain).astype(BF16)
-        return 0
-
-    lax.fori_loop(0, heads, attend, 0)
+        got = (attended * scale * gain).astype(BF16)
+        normed[:, group_cols(h0)] = jnp.concatenate([got[g] for g in range(GROUP)], axis=1)
+        return 0
+
+    lax.fori_loop(0, pairs, attend, 0)
 
     def push(src, dst, kind, c, recv, where):
         return pltpu.make_async_remote_copy(
@@ -372,6 +426,7 @@
         far_b(c).wait_recv()
         part[c, 1, left] = part[c, 1, left] + relay[c, 1]
         sum_b(c).start()
+        return 0
 
     def compute(c):
         load(c).wait()
@@ -382,18 +437,17 @@
         part[c, 1] = got[:, half:].reshape(ring, rows, half)
         far_a(c).start()
         far_b(c).start()
+        return 0
+
+    lax.fori_loop(0, chunks, lambda c, _: compute(c), 0)
+
+    def near(c, _):
         near_b(c).start()
         near_a(c).start()
-
-    compute(0)
-
-    def lap(c, _):
-        compute(c)
-        merge(c - 1)
-        return 0
-
-    lax.fori_loop(1, chunks, lap, 0)
-    merge(chunks - 1)
+        return 0
+
+    lax.fori_loop(0, chunks, near, 0)
+    lax.fori_loop(0, chunks, lambda c, _: merge(c), 0)
 
     @pl.when(at_end)
     def _():
@@ -401,9 +455,10 @@
             other = lax.rem(i + offset, heads)
             pltpu.make_async_copy(finals.at[other], finals.at[other], share_recv.at[other]).wait()
         for plane in range(planes):
-            total = finals[0] * pick_ref[plane, 0]
+            picked = owned(plane * heads + i)
+            total = finals[0] * picked[:, 0:1]
             for h in range(1, heads):
-                total = total + finals[h] * pick_ref[plane, h]
+                total = total + finals[h] * picked[:, h:h + 1]
             if plane < planes - 1:
                 chosen[plane] = total
                 give(plane).start()
@@ -435,9 +490,13 @@
     def _():
         give(0).wait_recv()
 
-    for step in range(heads - 1):
-        give_a(lax.rem(i + 1 + step, heads), step).wait_send()
-        give_c(step + 1).wait_send()
+    mine = owned(seq)
+    for h in range(heads):
+        states_ref[0, h] = taken[...] * mine[:, h:h + 1]
+
+    for offset in range(1, heads):
+        give_a(peer(offset)).wait_send()
+        give_c(offset).wait_send()
     for p in range(PIECES):
         for s in range(n_up):
             hop(s, p, True).wait_send()
@@ -445,9 +504,9 @@
             hop(s, p, False).wait_send()
 
 
-def whole(queries, keys, vals, beta_rates, log_gate, gain, out_weight, pick, ring, chunks=8):
+def whole(queries, keys, vals, beta_rates, log_gate, gain, out_weight, owner, planes, ring, chunks=8):
     tokens, wide = queries.shape
-    planes, heads = pick.shape
+    heads = owner.shape[1]
     nb = tokens // TB
     depth, columns = out_weight.shape
     width = columns // chunks
@@ -456,13 +515,24 @@
     dma = pltpu.SemaphoreType.DMA
     vmem = pl.BlockSpec(memory_space=pltpu.VMEM)
     outside = pl.BlockSpec(memory_space=pl.ANY)
+    hbm = pl.BlockSpec(memory_space=pltpu.HBM)
     pair = (heads, K, 2 * K)
     return pl.pallas_call(
         functools.partial(whole_kernel, planes),
-        in_specs=[outside, vmem, vmem, vmem, vmem, vmem, outside, pl.BlockSpec(memory_space=pltpu.SMEM)],
+        in_specs=[hbm, outside, outside, hbm, hbm, hbm, hbm, hbm],
         out_specs=[vmem, vmem],
-        out_shape=[jax.ShapeDtypeStruct((rows, columns), BF16), jax.ShapeDtypeStruct((K, K), F32)],
+        out_shape=[
+            jax.ShapeDtypeStruct((rows, columns), BF16),
+            jax.ShapeDtypeStruct((1, heads, K, K), F32),
+        ],
         scratch_shapes=[
+            pltpu.VMEM((K, K), F32),
+            pltpu.VMEM(owner.shape, jnp.int32),
+            pltpu.VMEM((1, K), F32),
+            pltpu.VMEM((2 * heads, tokens), F32),
+            pltpu.VMEM((heads, tokens), F32),
+            pltpu.VMEM((heads // GROUP, 2, tokens, GROUP * K), BF16),
+            pltpu.VMEM((heads // GROUP, 2, tokens, GROUP * K), BF16),
             pltpu.VMEM((tokens, wide), BF16),
             pltpu.VMEM((chunks, depth, width), BF16),
             pltpu.VMEM((tokens, heads), F32),
@@ -470,13 +540,13 @@
             pltpu.VMEM((tokens, 2 * heads), F32),
             pltpu.VMEM(pair, F32),
             pltpu.VMEM(pair, F32),
-            pltpu.VMEM((heads, nb, ROWS, 2 * K), BF16),
-            pltpu.VMEM((heads, nb, ROWS, 2 * K), BF16),
-            pltpu.VMEM((heads, nb, K, ROWS), BF16),
-            pltpu.VMEM((heads, nb, K, ROWS), BF16),
-            pltpu.VMEM((heads, nb - 1, K, 2 * K), F32),
-            pltpu.VMEM((tokens, wide), F32),
-            pltpu.VMEM((tokens, wide), F32),
+            pltpu.VMEM((heads // GROUP, GROUP * nb, ROWS, 2 * K), BF16),
+            pltpu.VMEM((heads // GROUP, GROUP * nb, ROWS, 2 * K), BF16),
+            pltpu.VMEM((heads // GROUP, GROUP * nb, K, ROWS), BF16),
+            pltpu.VMEM((heads // GROUP, GROUP * nb, K, ROWS), BF16),
+            pltpu.VMEM((heads // GROUP, nb - 1, GROUP, K, 2 * K), F32),
+            pltpu.VMEM((heads, tokens, K), F32),
+            pltpu.VMEM((heads, tokens, K), F32),
             pltpu.VMEM((n_up, K, 2 * K), F32),
             pltpu.VMEM((n_dn, K, 2 * K), F32),
             pltpu.VMEM((heads, K, K), F32),
@@ -488,17 +558,17 @@
             pltpu.VMEM((chunks, 4, rows, half), F32),
             pltpu.VMEM((heads, K, K), F32),
             pltpu.VMEM((planes - 1, K, K), F32),
-            dma((1,)), dma((chunks,)), dma((heads - 1,)), dma((heads,)),
+            dma((1,)), dma((4,)), dma((heads // GROUP, 2)), dma((chunks,)), dma((heads - 1,)), dma((heads,)),
             dma((n_up, PIECES)), dma((n_up, PIECES)), dma((n_dn, PIECES)), dma((n_dn, PIECES)),
             dma((heads - 1,)), dma((heads,)),
             dma((chunks, 6)), dma((chunks, 2)), dma((chunks, 4)),
             dma((heads - 1,)), dma((heads,)), dma((planes - 1,)), dma((1,)),
         ],
         compiler_params=pltpu.CompilerParams(
-            collective_id=1, has_side_effects=True, vmem_limit_bytes=50 * 1024 * 1024
+            collective_id=1, has_side_effects=True, vmem_limit_bytes=60 * 1024 * 1024
         ),
         name="whole",
-    )(queries, keys, vals, beta_rates, log_gate, gain, out_weight, pick)
+    )(queries, keys, vals, beta_rates, log_gate, gain, out_weight, owner)
 
 
 def per_device(
@@ -506,16 +576,10 @@
 ):
     heads = log_gate.shape[1]
     planes = lax.axis_size("seq") // heads
-    position = lax.axis_index("seq")
-    column = jnp.arange(planes) * heads + lax.rem(position, heads)
-    pick = jnp.any(decode_owner[None] == column[:, None, None], axis=1).astype(F32)
-    mixed, taken = whole(
+    return whole(
         queries, key_vectors.transpose(1, 0, 2), values.transpose(1, 0, 2), beta_rates.T, log_gate.T,
-        norm_gain.reshape(1, K), out_weight, pick, lax.axis_size("head"),
+        norm_gain.reshape(1, K), out_weight, decode_owner, planes, lax.axis_size("head"),
     )
-    owned = jnp.any(decode_owner == position, axis=0)
-    decode_states = jnp.where(owned[:, None, None], taken[None], 0.0)[None]
-    return mixed, decode_states
 
 
 def solution(mesh):

time: 110 us -> 107 us (0.973)
  other arithmetic: 2.37 us -> 0 us
  local copies, waits for them, and re-layouts: 6.07 us -> 7.26 us
    reduce_or x2 -> x0, other arithmetic: 1.46 us -> none  [the longest x1 0.75 us: per_device(): jnp.any(decode_owner[None] == column[:, None, None], axis=1).astype(F32)]
    transpose x1, local copies, waits for them, and re-layouts: 2.17 us -> 3.52 us  [per_device(): values.transpose(1, 0, 2)]
    pallas_call x1, Pallas kernels: 100 us -> 98.9 us  [whole(): pl.pallas_call(functools.partial(whole_kernel, planes), in_specs=[hbm, ou...]
    unnamed x9 -> x2, local copies, waits for them, and re-layouts: 3.9 us -> 3.74 us
where the time goes in v3:
time: 107 us
  Pallas kernels  98.9 us (92%)
  local copies, waits for them, and re-layouts  7.26 us (7%)
    pallas_call x1, Pallas kernels, whole(): pl.pallas_call(functools.partial(whole_kernel, planes), in_specs=[hbm, ou...  98.9 us
    unnamed x2, local copies, waits for them, and re-layouts  3.74 us
    transpose x1, local copies, waits for them, and re-layouts, per_device(): values.transpose(1, 0, 2)  3.52 us

profile of v3, /device:TPU:1, one launch (start us, length us, event | category | flops | bytes accessed | tf_op | source)
XLA Modules:
  0.0 106.8 jit_solution(17535847725362796618)
XLA Ops:
  0.6 3.5 %copy_bitcast_fusion = (bf16[2,256,1024]{2,1,0:T(8,128)(2,1)}, bf16[2,256,1024]{2,1,0:T(8,128)(2,1)}) fusion(bf16[256,2,1024]{2,1,0:T(2,128)(2,1)} %param.10, bf16[256,2,1024]{2,1,0:T(2,128)(2,1)} %param.9), kind=kLoop, calls=%fused_computation | loop fusion | bytes 4194304 | tf_op jit(solution)/shard_map/transpose | solution.py:580
  4.2 98.9 %whole.1 = (bf16[64,4096]{1,0:T(8,128)(2,1)}, f32[1,8,128,128]{3,2,1,0:T(8,128)}) custom-call(bf16[256,1024]{1,0:T(8,128)(2,1)} %q_ref.1, bf16[2,256,1024]{2,1,0:T(8,128)(2,1)} %get-tuple-element.3.k_hbm, bf16[2,256,1024]{2,1,0:T(8,128)(2,1)} %get-tuple-element.2.v_hbm, f32[16,256]{1,0:T(8,128)} %bitcast.7, f32[8,256]{1,0:T(8,128)} %bitcast.8, ...), custom_call_target="tpu_custom_call" | custom-call | tf_op jit(solution)/shard_map/whole/pallas_call | solution.py:520
  103.1 1.9 %copy.16 = bf16[64,4096]{1,0:T(8,128)(2,1)} copy(bf16[64,4096]{1,0:T(8,128)(2,1)} %get-tuple-element.6) | data formatting | bytes 1048576
  104.9 1.9 %copy.17 = f32[1,8,128,128]{3,2,1,0:T(8,128)} copy(f32[1,8,128,128]{3,2,1,0:T(8,128)} %get-tuple-element.7) | data formatting | bytes 1048576

commit v4 on v3

--- a/solution.py
+++ b/solution.py
@@ -39,7 +39,7 @@
 
 MESH = pl.DeviceIdType.MESH
 PIECES = 2
-GROUP = 2
+GROUP = 4
 
 
 def place(wide_c):
@@ -54,6 +54,23 @@
 def decays(run, run_lane):
     seen = iota((TB, ROWS), 1) % TB <= iota((TB, ROWS), 0)
     return jnp.where(seen, jnp.exp(jnp.where(seen, run - run_lane, 0.0)), 0.0)
+
+
+def odd_rows(x, size, which=1):
+    groups = x.reshape(x.shape[0], ROWS // (2 * size), 2, size, x.shape[-1])
+    return groups[:, :, which].reshape(x.shape[0], ROWS // 2, x.shape[-1])
+
+
+def among_odd(odd, even, size):
+    shape = (odd.shape[0], ROWS // (2 * size), 1, size, odd.shape[-1])
+    both = jnp.concatenate([even.reshape(shape), odd.reshape(shape)], axis=2)
+    return both.reshape(odd.shape[0], ROWS, odd.shape[-1])
+
+
+def three(x):
+    one = x.astype(BF16).astype(F32)
+    two = (x - one).astype(BF16).astype(F32)
+    return [one, two, x - one - two]
 
 
 def invert(system, nb, r_t, s_t):
@@ -80,21 +97,24 @@
     size = SUB
     while size < TB:
         pair = ((r_t // (2 * size)) == (s_t // (2 * size))) & ((r_t // size) > (s_t // size))
-        parts = split(solve)
-        solve = solve - mm3(parts, mm3(jnp.where(pair, system, 0.0), parts))
+        later = odd_rows(solve, size)
+        crossed = mm3(odd_rows(jnp.where(pair, system, 0.0), size), solve)
+        later = later - mm3(later, among_odd(crossed, jnp.zeros_like(crossed), size))
+        solve = among_odd(later, odd_rows(solve, size, 0), size)
         size *= 2
     return solve
 
 
 def whole_kernel(
-    planes, q_ref, k_hbm, v_hbm, beta_hbm, gate_hbm, gain_hbm, w_ref, owner_hbm,
-    out_ref, states_ref, taken, owner_ref, gain_ref, beta_ref, gate_ref, k_ref, v_ref, q_buf, w_buf, run_scr, row_scr, beta_scr, sp, gath, rows_hi, rows_lo,
+    planes, q_ref, k_hbm, v_hbm, small_ref, w_ref,
+    out_ref, states_ref, taken, k_ref, v_ref, q_buf, w_buf, col_scr, row_scr, sp, gath, rows_hi, rows_lo,
     kt_hi, kt_lo, carry, reach_scr, base_scr, from_low, from_high, out_buf, in_buf, end_buf,
     normed, part, relay, landed, finals, chosen,
-    q_sem, in_sem, k_sem, w_sem, send_a, recv_a, send_up, recv_up, send_dn, recv_dn, send_c, recv_c,
+    q_sem, k_sem, w_sem, send_a, recv_a, send_up, recv_up, send_dn, recv_dn, send_c, recv_c,
     send_sem, relay_sem, land_sem, share_send, share_recv, give_send, give_recv,
 ):
-    heads, tokens = gate_ref.shape
+    tokens = small_ref.shape[1]
+    heads = sp.shape[0]
     nb = tokens // TB
     chunks, depth, width = w_buf.shape
     half = width // 2
@@ -116,29 +136,21 @@
         return pltpu.make_async_copy(w_ref.at[:, pl.ds(c * width, width)], w_buf.at[c], w_sem.at[c])
 
     q_load = pltpu.make_async_copy(q_ref, q_buf, q_sem.at[0])
-    small = [
-        pltpu.make_async_copy(src, dst, in_sem.at[n])
-        for n, (src, dst) in enumerate(
-            [(gate_hbm, gate_ref), (beta_hbm, beta_ref), (gain_hbm, gain_ref), (owner_hbm, owner_ref)]
-        )
-    ]
     pairs = heads // GROUP
 
-    def load_pair(n):
-        pair = lax.rem(i // GROUP + 1 + n, pairs)
-        lanes = pl.ds(pl.multiple_of(pair * GROUP * K, GROUP * K), GROUP * K)
+    def load_head(h):
+        dst = pl.ds(h // pairs * K, K)
         return [
-            pltpu.make_async_copy(src.at[:, :, lanes], dst.at[pair], k_sem.at[n, j])
-            for j, (src, dst) in enumerate([(k_hbm, k_ref), (v_hbm, v_ref)])
+            pltpu.make_async_copy(
+                src.at[:, :, pl.ds(h * K, K)], buf.at[h % pairs, :, :, dst], k_sem.at[h % pairs, h // pairs, j]
+            )
+            for j, (src, buf) in enumerate([(k_hbm, k_ref), (v_hbm, v_ref)])
         ]
 
-    for copy in small[:2]:
-        copy.start()
     for n in range(pairs):
-        for copy in load_pair(n):
-            copy.start()
-    for copy in small[2:]:
-        copy.start()
+        for g in range(GROUP):
+            for copy in load_head(n + pairs * g):
+                copy.start()
     q_load.start()
     for c in range(chunks):
         load(c).start()
@@ -154,46 +166,49 @@
         source = (planes - 1) * heads + i
         pl.semaphore_signal(barrier, inc=1, device_id=(source, me), device_id_type=MESH)
 
-    for copy in small:
-        copy.wait()
-    gate = gate_ref[...]
+    gate = small_ref[0:heads]
     t_i, s_i = iota((tokens, tokens), 0), iota((tokens, tokens), 1)
     upto = jnp.where(((t_i // TB) == (s_i // TB)) & (s_i <= t_i), 1.0, 0.0).astype(F32)
-    run_scr[...] = lax.dot_general(
-        upto, gate, (((1,), (1,)), ((), ())), precision=lax.Precision.HIGHEST, preferred_element_type=F32
+    run = lax.dot_general(
+        gate, upto, (((1,), (1,)), ((), ())), precision=lax.Precision.HIGHEST, preferred_element_type=F32
     )
-    t_j, l_j = iota((tokens, nb * ROWS), 0), iota((tokens, nb * ROWS), 1)
-    spread = jnp.where(((t_j // TB) == (l_j // ROWS)) & ((t_j % TB) <= (l_j % TB)), 1.0, 0.0).astype(F32)
-    row_scr[...] = lax.dot_general(
-        gate, spread, (((1,), (0,)), ((), ())), precision=lax.Precision.HIGHEST, preferred_element_type=F32
+    terms = jnp.concatenate(three(small_ref[heads:3 * heads]) + three(run), axis=0).astype(BF16)
+    same = jnp.where(t_i == s_i, 1.0, 0.0).astype(BF16)
+    col_scr[...] = lax.dot_general(
+        same, terms, (((1,), (1,)), ((), ())), preferred_element_type=F32
+    ).astype(BF16)
+    row_scr[...] = jnp.concatenate(
+        [run[:, b // 2 * TB:(b // 2 + 1) * TB] for b in range(2 * nb)], axis=1
     )
-    same = jnp.where(t_i == s_i, 1.0, 0.0).astype(F32)
-    beta_scr[...] = lax.dot_general(
-        same, beta_ref[...], (((1,), (1,)), ((), ())), precision=lax.Precision.HIGHEST,
-        preferred_element_type=F32,
-    )
 
     batch = GROUP * nb
 
-    def column(ref, lanes_at):
-        lanes = iota(ref.shape, 1)
-        got = [
-            jnp.sum(jnp.where(lanes == at, ref[...], 0.0), axis=1, keepdims=True).reshape(nb, TB, 1)
-            for at in lanes_at
-        ]
-        return jnp.concatenate(got, axis=0)
+    def columns(h0, kinds):
+        shape = (9 * heads, K)
+        at = iota(shape, 0)
+        rate_at, run_at = jnp.where(at < 6 * heads, at % (2 * heads), -1), jnp.where(at < 6 * heads, -1, at % heads)
+        picks = []
+        for kind in kinds:
+            for g in range(GROUP):
+                hit = (run_at == h0 + pairs * g) if kind == 2 else (rate_at == 2 * (h0 + pairs * g) + kind)
+                picks.append(jnp.where(hit, 1.0, 0.0).astype(BF16))
+        got = lax.dot_general(
+            col_scr[...], jnp.concatenate(picks, axis=1), (((1,), (0,)), ((), ())), preferred_element_type=F32
+        )
+        tiles = [got[:, n * K:(n + 1) * K].reshape(nb, TB, K) for n in range(len(picks))]
+        return [jnp.concatenate(tiles[n:n + GROUP], axis=0) for n in range(0, len(picks), GROUP)]
 
     def lane_rows(h0):
         got = []
         for g in range(GROUP):
             picked = jnp.sum(
-                jnp.where(iota((heads, nb * ROWS), 0) == h0 + g, row_scr[...], 0.0), axis=0, keepdims=True
+                jnp.where(iota((heads, nb * ROWS), 0) == h0 + pairs * g, row_scr[...], 0.0), axis=0, keepdims=True
             )
             got += [picked[:, b * ROWS:(b + 1) * ROWS] for b in range(nb)]
         return jnp.stack(got, axis=0)
 
-    def group_cols(h0):
-        return pl.ds(pl.multiple_of(h0 * K, GROUP * K), GROUP * K)
+    def head_cols(h):
+        return pl.ds(pl.multiple_of(h * K, K), K)
 
     def by_head(x):
         return jnp.concatenate([x[:, g * K:(g + 1) * K].reshape(nb, TB, K) for g in range(GROUP)], axis=0)
@@ -209,17 +224,15 @@
         )
 
     def transition(step, _):
-        pair = lax.rem(i // GROUP + 1 + step, pairs)
-        h0 = pair * GROUP
-        for src, j in ((k_hbm, 0), (v_hbm, 1)):
-            dst = (k_ref, v_ref)[j]
-            pltpu.make_async_copy(dst.at[pair], dst.at[pair], k_sem.at[step, j]).wait()
-        run = column(run_scr, [h0 + g for g in range(GROUP)])
+        pair = h0 = step
+        for g in range(GROUP):
+            for j, buf in enumerate((k_ref, v_ref)):
+                here = buf.at[pair, :, :, pl.ds(g * K, K)]
+                pltpu.make_async_copy(here, here, k_sem.at[pair, g, j]).wait()
+        rate0, rate1, run = columns(h0, (0, 1, 2))
         run_lane = lane_rows(h0)
         closing = run_lane[:, :, ROWS - 1:ROWS]
-        rates = jnp.concatenate(
-            [column(beta_scr, [2 * (h0 + g) + j for g in range(GROUP)]) for j in range(2)], axis=1
-        )
+        rates = jnp.concatenate([rate0, rate1], axis=1)
         key = unit(jnp.concatenate([by_head(k_ref[pair, j].astype(F32)) for j in range(2)], axis=1))
         val = jnp.concatenate([by_head(v_ref[pair, j].astype(F32)) for j in range(2)], axis=1)
         key_t = jnp.stack([key[b].T for b in range(batch)], axis=0)
@@ -243,7 +256,8 @@
         for b in range(1, nb):
             carry[pair, b - 1] = state
             state = mm3(move[:, b], state) + place(fresh[:, b])
-        sp[pl.ds(h0, GROUP)] = state
+        for g in range(GROUP):
+            sp[h0 + pairs * g] = state[g]
 
         @pl.when((step == 0) & at_end)
         def _():
@@ -254,11 +268,11 @@
             pl.semaphore_wait(barrier, heads + 3)
 
         for g in range(GROUP):
-            @pl.when(h0 + g != i)
+            @pl.when(h0 + pairs * g != i)
             def _():
-                give_a(h0 + g).start()
-
-            @pl.when(h0 + g == i)
+                give_a(h0 + pairs * g).start()
+
+            @pl.when(h0 + pairs * g == i)
             def _():
                 gath[i] = state[g]
 
@@ -267,9 +281,11 @@
     lax.fori_loop(0, pairs, transition, 0)
 
     def reaches(pair, _):
-        h0 = pair * GROUP
-        run = column(run_scr, [h0 + g for g in range(GROUP)])
-        query = by_head(q_buf[:, group_cols(h0)].astype(F32))
+        h0 = pair
+        (run,) = columns(h0, (2,))
+        query = jnp.concatenate(
+            [q_buf[:, head_cols(h0 + pairs * g)].astype(F32).reshape(nb, TB, K) for g in range(GROUP)], axis=0
+        )
         scores = mm3(query, (kt_hi[pair], kt_lo[pair])) * decays(run, lane_rows(h0))
         z_out = mm3(scores, (rows_hi[pair], rows_lo[pair])).reshape(GROUP, nb, TB, 2 * K)
         reach = (jnp.exp(run) * query).reshape(GROUP, nb, TB, K) - z_out[..., K:]
@@ -279,10 +295,13 @@
             both = mm3(reach[:, b], carry[pair, b - 1])
             base.append(both[:, :, :K] + z_out[:, b, :, :K])
             whole_reach.append(both[:, :, K:])
-        base_scr[pl.ds(h0, GROUP)] = jnp.concatenate(base, axis=1)
-        reach_scr[pl.ds(h0, GROUP)] = jnp.concatenate(whole_reach, axis=1)
+        base_scr[pair] = jnp.concatenate(base, axis=1)
+        reach_scr[pair] = jnp.concatenate(whole_reach, axis=1)
         return 0
 
+    early = jnp.where(lax.rem(i, pairs) == 0, 0, pairs)
+    q_load.wait()
+    lax.fori_loop(0, early, reaches, 0)
     for src in range(heads):
         @pl.when(src != i)
         def _():
@@ -311,13 +330,12 @@
     for p in range(PIECES):
         hop(0, p, True).start()
         hop(0, p, False).start()
-    q_load.wait()
     k_i, k_j = iota((K, 2 * K), 0), iota((K, 2 * K), 1)
     acc = jnp.where(k_i + K == k_j, 1.0, 0.0).astype(F32)
     state = jnp.zeros((K, K), F32)
-    each = pairs // n_up
     for s in range(n_up):
-        lax.fori_loop(s * each, (s + 1) * each, reaches, 0)
+        if s == 0:
+            lax.fori_loop(early, pairs, reaches, 0)
         for p in range(PIECES):
             hop(s, p, True).wait_recv()
             if s + 1 < n_up:
@@ -344,7 +362,7 @@
     def give_c(offset):
         other = peer(offset)
         return pltpu.make_async_remote_copy(
-            src_ref=out_buf.at[other], dst_ref=in_buf.at[i], send_sem=send_c.at[offset - 1],
+            src_ref=out_buf.at[other], dst_ref=in_buf.at[lax.rem(i, pairs), i // pairs], send_sem=send_c.at[offset - 1],
             recv_sem=recv_c.at[i], device_id=(z * heads + other, me), device_id_type=MESH,
         )
 
@@ -363,7 +381,7 @@
 
     for offset in range(1, heads):
         give_c(offset).start()
-    in_buf[i] = out_buf[i]
+    in_buf[lax.rem(i, pairs), i // pairs] = out_buf[i]
 
     @pl.when(at_end)
     def _():
@@ -371,26 +389,28 @@
         for offset in range(1, heads):
             share(offset).start()
 
-    gain = gain_ref[...]
+    gain = small_ref[3 * heads:3 * heads + 1, 0:K]
 
     def owned(device):
-        found = jnp.where(owner_ref[...] == device, 1.0, 0.0).astype(F32)
+        owners = small_ref[3 * heads + 1:3 * heads + 3, 0:heads]
+        found = jnp.where(owners == lax.convert_element_type(device, F32), 1.0, 0.0).astype(F32)
         return jnp.max(found, axis=0, keepdims=True)
 
 
     def attend(step, _):
-        pair = lax.rem(i // GROUP + step, pairs)
-        h0 = pair * GROUP
         for g in range(GROUP):
-            @pl.when(h0 + g != i)
+            h = step + pairs * g
+
+            @pl.when(h != i)
             def _():
-                pltpu.make_async_copy(in_buf.at[h0 + g], in_buf.at[h0 + g], recv_c.at[h0 + g]).wait()
-
-        these = pl.ds(h0, GROUP)
-        attended = base_scr[these] + mm3(reach_scr[these], in_buf[these])
+                here = in_buf.at[step, g]
+                pltpu.make_async_copy(here, here, recv_c.at[h]).wait()
+
+        attended = base_scr[step] + mm3(reach_scr[step], in_buf[step])
         scale = lax.rsqrt(jnp.mean(attended * attended, axis=-1, keepdims=True) + 1e-6)
         got = (attended * scale * gain).astype(BF16)
-        normed[:, group_cols(h0)] = jnp.concatenate([got[g] for g in range(GROUP)], axis=1)
+        for g in range(GROUP):
+            normed[:, head_cols(step + pairs * g)] = got[g]
         return 0
 
     lax.fori_loop(0, pairs, attend, 0)
@@ -504,9 +524,8 @@
             hop(s, p, False).wait_send()
 
 
-def whole(queries, keys, vals, beta_rates, log_gate, gain, out_weight, owner, planes, ring, chunks=8):
+def whole(queries, keys, vals, small, out_weight, heads, planes, ring, chunks=8):
     tokens, wide = queries.shape
-    heads = owner.shape[1]
     nb = tokens // TB
     depth, columns = out_weight.shape
     width = columns // chunks
@@ -519,7 +538,7 @@
     pair = (heads, K, 2 * K)
     return pl.pallas_call(
         functools.partial(whole_kernel, planes),
-        in_specs=[hbm, outside, outside, hbm, hbm, hbm, hbm, hbm],
+        in_specs=[hbm, outside, outside, vmem, hbm],
         out_specs=[vmem, vmem],
         out_shape=[
             jax.ShapeDtypeStruct((rows, columns), BF16),
@@ -527,17 +546,12 @@
         ],
         scratch_shapes=[
             pltpu.VMEM((K, K), F32),
-            pltpu.VMEM(owner.shape, jnp.int32),
-            pltpu.VMEM((1, K), F32),
-            pltpu.VMEM((2 * heads, tokens), F32),
-            pltpu.VMEM((heads, tokens), F32),
             pltpu.VMEM((heads // GROUP, 2, tokens, GROUP * K), BF16),
             pltpu.VMEM((heads // GROUP, 2, tokens, GROUP * K), BF16),
             pltpu.VMEM((tokens, wide), BF16),
             pltpu.VMEM((chunks, depth, width), BF16),
-            pltpu.VMEM((tokens, heads), F32),
+            pltpu.VMEM((tokens, 9 * heads), BF16),
             pltpu.VMEM((heads, nb * ROWS), F32),
-            pltpu.VMEM((tokens, 2 * heads), F32),
             pltpu.VMEM(pair, F32),
             pltpu.VMEM(pair, F32),
             pltpu.VMEM((heads // GROUP, GROUP * nb, ROWS, 2 * K), BF16),
@@ -545,12 +559,12 @@
             pltpu.VMEM((heads // GROUP, GROUP * nb, K, ROWS), BF16),
             pltpu.VMEM((heads // GROUP, GROUP * nb, K, ROWS), BF16),
             pltpu.VMEM((heads // GROUP, nb - 1, GROUP, K, 2 * K), F32),
-            pltpu.VMEM((heads, tokens, K), F32),
-            pltpu.VMEM((heads, tokens, K), F32),
+            pltpu.VMEM((heads // GROUP, GROUP, tokens, K), F32),
+            pltpu.VMEM((heads // GROUP, GROUP, tokens, K), F32),
             pltpu.VMEM((n_up, K, 2 * K), F32),
             pltpu.VMEM((n_dn, K, 2 * K), F32),
             pltpu.VMEM((heads, K, K), F32),
-            pltpu.VMEM((heads, K, K), F32),
+            pltpu.VMEM((heads // GROUP, GROUP, K, K), F32),
             pltpu.VMEM((K, K), F32),
             pltpu.VMEM((tokens, depth), BF16),
             pltpu.VMEM((chunks, 2, ring, rows, half), F32),
@@ -558,17 +572,17 @@
             pltpu.VMEM((chunks, 4, rows, half), F32),
             pltpu.VMEM((heads, K, K), F32),
             pltpu.VMEM((planes - 1, K, K), F32),
-            dma((1,)), dma((4,)), dma((heads // GROUP, 2)), dma((chunks,)), dma((heads - 1,)), dma((heads,)),
+            dma((1,)), dma((heads // GROUP, GROUP, 2)), dma((chunks,)), dma((heads - 1,)), dma((heads,)),
             dma((n_up, PIECES)), dma((n_up, PIECES)), dma((n_dn, PIECES)), dma((n_dn, PIECES)),
             dma((heads - 1,)), dma((heads,)),
             dma((chunks, 6)), dma((chunks, 2)), dma((chunks, 4)),
             dma((heads - 1,)), dma((heads,)), dma((planes - 1,)), dma((1,)),
         ],
         compiler_params=pltpu.CompilerParams(
-            collective_id=1, has_side_effects=True, vmem_limit_bytes=60 * 1024 * 1024
+            collective_id=1, has_side_effects=True, vmem_limit_bytes=50 * 1024 * 1024
         ),
         name="whole",
-    )(queries, keys, vals, beta_rates, log_gate, gain, out_weight, owner)
+    )(queries, keys, vals, small, out_weight)
 
 
 def per_device(
@@ -576,9 +590,19 @@
 ):
     heads = log_gate.shape[1]
     planes = lax.axis_size("seq") // heads
+    tokens = queries.shape[0]
+    small = jnp.concatenate(
+        [
+            log_gate.T, beta_rates.T,
+            jnp.pad(norm_gain.reshape(1, K), ((0, 0), (0, tokens - K))),
+            jnp.pad(decode_owner.astype(F32), ((0, 0), (0, tokens - heads))),
+            jnp.zeros((5, tokens), F32),
+        ],
+        axis=0,
+    )
     return whole(
-        queries, key_vectors.transpose(1, 0, 2), values.transpose(1, 0, 2), beta_rates.T, log_gate.T,
-        norm_gain.reshape(1, K), out_weight, decode_owner, planes, lax.axis_size("head"),
+        queries, key_vectors.transpose(1, 0, 2), values.transpose(1, 0, 2), small, out_weight,
+        heads, planes, lax.axis_size("head"),
     )
 
 

time: 107 us -> 96.9 us (0.906)
  Pallas kernels: 98.9 us -> 88.3 us
    pallas_call x1, Pallas kernels: 98.9 us -> 88.3 us  [whole(): pl.pallas_call(functools.partial(whole_kernel, planes), in_specs=[hbm, ou...]
    concatenate x0 -> x1, local copies, waits for them, and re-layouts: none -> 1.44 us  [per_device(): jnp.concatenate([log_gate.T, beta_rates.T, jnp.pad(norm_gain.reshape(1, K...]
    transpose x1, local copies, waits for them, and re-layouts: 3.52 us -> 2.17 us  [per_device(): values.transpose(1, 0, 2)]
    unnamed x2 -> x4, local copies, waits for them, and re-layouts: 3.74 us -> 2.63 us
where the time goes in v4:
time: 96.9 us; the launch traced here: 96.6 us
  Pallas kernels  88.3 us (91%)
  local copies, waits for them, and re-layouts  6.9 us (7%)
    pallas_call x1, Pallas kernels, whole(): pl.pallas_call(functools.partial(whole_kernel, planes), in_specs=[hbm, ou...  88.3 us
    unnamed x4, local copies, waits for them, and re-layouts  2.63 us
    transpose x1, local copies, waits for them, and re-layouts, per_device(): values.transpose(1, 0, 2)  2.17 us

profile of v4, /device:TPU:1, one launch (start us, length us, event | category | flops | bytes accessed | tf_op | source)
XLA Modules:
  0.0 96.6 jit_solution(3938925837830420531)
XLA Ops:
  0.6 0.7 pad.8
  1.3 0.7 convert_element_type.7
  2.0 1.4 %concatenate.3.small_ref = f32[32,256]{1,0:T(8,128)S(1)} concatenate(f32[8,256]{1,0:T(8,128)} %bitcast.8, f32[16,256]{1,0:T(8,128)} %bitcast.7, f32[1,256]{1,0:T(1,128)S(1)} %pad.8, f32[2,256]{1,0:T(2,128)S(1)} %pad.9, f32[5,256]{1,0:T(8,128)S(1)} %broadcast_in_dim.3), dimensions={0} | concatenate | bytes 65536 | tf_op jit(solution)/shard_map/concatenate | solution.py:594
  3.4 2.2 %copy_bitcast_fusion = (bf16[2,256,1024]{2,1,0:T(8,128)(2,1)S(1)}, bf16[2,256,1024]{2,1,0:T(8,128)(2,1)S(1)}) fusion(bf16[256,2,1024]{2,1,0:T(2,128)(2,1)} %param.10, bf16[256,2,1024]{2,1,0:T(2,128)(2,1)} %param.9), kind=kLoop, calls=%fused_computation | loop fusion | bytes 4194304 | tf_op jit(solution)/shard_map/transpose | solution.py:604
  5.6 0.0 copy-start
  5.6 1.0 %copy-done = bf16[256,1024]{1,0:T(8,128)(2,1)S(1)} copy-done((bf16[256,1024]{1,0:T(8,128)(2,1)S(1)}, bf16[256,1024]{1,0:T(8,128)(2,1)}, u32[]{:S(2)}) %copy-start) | copy-done | bytes 524312
  6.6 88.3 %whole.1 = (bf16[64,4096]{1,0:T(8,128)(2,1)S(1)}, f32[1,8,128,128]{3,2,1,0:T(8,128)S(1)}) custom-call(bf16[256,1024]{1,0:T(8,128)(2,1)S(1)} %copy-done, bf16[2,256,1024]{2,1,0:T(8,128)(2,1)S(1)} %get-tuple-element.3.k_hbm, bf16[2,256,1024]{2,1,0:T(8,128)(2,1)S(1)} %get-tuple-element.2.v_hbm, f32[32,256]{1,0:T(8,128)S(1)} %concatenate.3.small_ref, ...), custom_call_target="tpu_custom_call" | custom-call | tf_op jit(solution)/shard_map/whole/pallas_call | solution.py:539
  95.0 0.8 copy.16
  95.8 0.8 copy.17
  (2 shorter events, 0.0 us)
Async XLA Ops:
  5.6 1.0 %copy-start = (bf16[256,1024]{1,0:T(8,128)(2,1)S(1)}, bf16[256,1024]{1,0:T(8,128)(2,1)}, u32[]{:S(2)}) copy-start(bf16[256,1024]{1,0:T(8,128)(2,1)} %q_ref.1) | copy-start | bytes 1572868

commit v5 on v4

--- a/solution.py
+++ b/solution.py
@@ -28,9 +28,19 @@
 def mm3(a, b):
     ah, al = a if isinstance(a, tuple) else split(a)
     bh, bl = b if isinstance(b, tuple) else split(b)
-    wide = jnp.concatenate([ah, al], axis=-1)
-    tall = jnp.concatenate([bh, bh], axis=-2)
-    return bdot(wide, tall) + bdot(ah, bl)
+    wide = jnp.concatenate([ah, al, ah], axis=-1)
+    tall = jnp.concatenate([bh, bh, bl], axis=-2)
+    return bdot(wide, tall)
+
+
+def twin(a, b):
+    n, m, k = a.shape
+    ah, al = split(a)
+    bh, bl = b if isinstance(b, tuple) else split(b)
+    wide = jnp.concatenate([ah, al, ah], axis=-1).reshape(n // 2, 2 * m, 3 * k)
+    bh, bl = [jnp.concatenate([x.reshape(n // 2, 2, k, k)[:, t] for t in range(2)], axis=-1) for x in (bh, bl)]
+    got = bdot(wide, jnp.concatenate([bh, bh, bl], axis=-2))
+    return jnp.stack([got[:, :m, :k], got[:, m:, k:]], axis=1).reshape(n, m, k)
 
 
 def iota(shape, dim):
@@ -98,19 +108,19 @@
     while size < TB:
         pair = ((r_t // (2 * size)) == (s_t // (2 * size))) & ((r_t // size) > (s_t // size))
         later = odd_rows(solve, size)
-        crossed = mm3(odd_rows(jnp.where(pair, system, 0.0), size), solve)
-        later = later - mm3(later, among_odd(crossed, jnp.zeros_like(crossed), size))
+        crossed = twin(odd_rows(jnp.where(pair, system, 0.0), size), solve)
+        later = later - twin(later, among_odd(crossed, jnp.zeros_like(crossed), size))
         solve = among_odd(later, odd_rows(solve, size, 0), size)
         size *= 2
     return solve
 
 
 def whole_kernel(
-    planes, q_ref, k_hbm, v_hbm, small_ref, w_ref,
-    out_ref, states_ref, taken, k_ref, v_ref, q_buf, w_buf, col_scr, row_scr, sp, gath, rows_hi, rows_lo,
+    planes, q_buf, k_ref, v_ref, small_ref, w_ref,
+    out_ref, states_ref, taken, w_buf, col_scr, row_scr, sp, total_buf, gath, rows_hi, rows_lo,
     kt_hi, kt_lo, carry, reach_scr, base_scr, from_low, from_high, out_buf, in_buf, end_buf,
     normed, part, relay, landed, finals, chosen,
-    q_sem, k_sem, w_sem, send_a, recv_a, send_up, recv_up, send_dn, recv_dn, send_c, recv_c,
+    w_sem, send_a, recv_a, send_up, recv_up, send_dn, recv_dn, send_c, recv_c,
     send_sem, relay_sem, land_sem, share_send, share_recv, give_send, give_recv,
 ):
     tokens = small_ref.shape[1]
@@ -135,23 +145,8 @@
     def load(c):
         return pltpu.make_async_copy(w_ref.at[:, pl.ds(c * width, width)], w_buf.at[c], w_sem.at[c])
 
-    q_load = pltpu.make_async_copy(q_ref, q_buf, q_sem.at[0])
     pairs = heads // GROUP
 
-    def load_head(h):
-        dst = pl.ds(h // pairs * K, K)
-        return [
-            pltpu.make_async_copy(
-                src.at[:, :, pl.ds(h * K, K)], buf.at[h % pairs, :, :, dst], k_sem.at[h % pairs, h // pairs, j]
-            )
-            for j, (src, buf) in enumerate([(k_hbm, k_ref), (v_hbm, v_ref)])
-        ]
-
-    for n in range(pairs):
-        for g in range(GROUP):
-            for copy in load_head(n + pairs * g):
-                copy.start()
-    q_load.start()
     for c in range(chunks):
         load(c).start()
 
@@ -210,8 +205,10 @@
     def head_cols(h):
         return pl.ds(pl.multiple_of(h * K, K), K)
 
-    def by_head(x):
-        return jnp.concatenate([x[:, g * K:(g + 1) * K].reshape(nb, TB, K) for g in range(GROUP)], axis=0)
+    def by_head(ref, h0):
+        return jnp.concatenate(
+            [ref[:, head_cols(h0 + pairs * g)].astype(F32).reshape(nb, TB, K) for g in range(GROUP)], axis=0
+        )
 
     def unit(x):
         return x * lax.rsqrt(jnp.sum(x * x, axis=-1, keepdims=True) + 1e-6)
@@ -225,23 +222,19 @@
 
     def transition(step, _):
         pair = h0 = step
-        for g in range(GROUP):
-            for j, buf in enumerate((k_ref, v_ref)):
-                here = buf.at[pair, :, :, pl.ds(g * K, K)]
-                pltpu.make_async_copy(here, here, k_sem.at[pair, g, j]).wait()
         rate0, rate1, run = columns(h0, (0, 1, 2))
         run_lane = lane_rows(h0)
         closing = run_lane[:, :, ROWS - 1:ROWS]
         rates = jnp.concatenate([rate0, rate1], axis=1)
-        key = unit(jnp.concatenate([by_head(k_ref[pair, j].astype(F32)) for j in range(2)], axis=1))
-        val = jnp.concatenate([by_head(v_ref[pair, j].astype(F32)) for j in range(2)], axis=1)
+        key = unit(jnp.concatenate([by_head(k_ref.at[j], h0) for j in range(2)], axis=1))
+        val = jnp.concatenate([by_head(v_ref.at[j], h0) for j in range(2)], axis=1)
         key_t = jnp.stack([key[b].T for b in range(batch)], axis=0)
         kth, ktl = split(key_t)
         kt_hi[pair], kt_lo[pair] = kth, ktl
         decay = decays(run, run_lane)
         r_i, s_i, r_t, s_t = masks()
         below = (r_t > s_t) | ((r_t == s_t) & (r_i > s_i))
-        gram = mm3(key, (kth, ktl))
+        gram = twin(key, (kth, ktl))
         system = jnp.where(below, rates * jnp.concatenate([decay, decay], axis=1) * gram, 0.0)
         solve = invert(system, batch, r_t, s_t)
         grown = jnp.exp(jnp.concatenate([run, run], axis=1))
@@ -283,9 +276,7 @@
     def reaches(pair, _):
         h0 = pair
         (run,) = columns(h0, (2,))
-        query = jnp.concatenate(
-            [q_buf[:, head_cols(h0 + pairs * g)].astype(F32).reshape(nb, TB, K) for g in range(GROUP)], axis=0
-        )
+        query = by_head(q_buf, h0)
         scores = mm3(query, (kt_hi[pair], kt_lo[pair])) * decays(run, lane_rows(h0))
         z_out = mm3(scores, (rows_hi[pair], rows_lo[pair])).reshape(GROUP, nb, TB, 2 * K)
         reach = (jnp.exp(run) * query).reshape(GROUP, nb, TB, K) - z_out[..., K:]
@@ -300,26 +291,24 @@
         return 0
 
     early = jnp.where(lax.rem(i, pairs) == 0, 0, pairs)
-    q_load.wait()
     lax.fori_loop(0, early, reaches, 0)
     for src in range(heads):
         @pl.when(src != i)
         def _():
             pltpu.make_async_copy(gath.at[src], gath.at[src], recv_a.at[src]).wait()
-    size = 1
-    while size < heads:
-        for begin in range(0, heads, 2 * size):
-            lo, hi = begin + size, begin + 2 * size
-            later = gath[lo:hi]
-            joined = mm3(later[:, :, K:].reshape(size * K, K), gath[lo - 1]).reshape(size, K, 2 * K)
-            gath[lo:hi] = joined + place(later[:, :, :K])
-        size *= 2
+    def compose(later, earlier):
+        return mm3(later[..., K:], earlier) + place(later[..., :K])
+
+    odd = gath[1], gath[3], gath[5], gath[7]
+    twos = compose(jnp.stack(odd), jnp.stack([gath[0], gath[2], gath[4], gath[6]]))
+    fours = compose(jnp.stack([twos[1], twos[3]]), jnp.stack([twos[0], twos[2]]))
+    total_buf[...] = compose(fours[1], fours[0])
 
     bit = K // PIECES
 
     def hop(s, p, upward):
         slots = from_low if upward else from_high
-        src = gath.at[heads - 1] if s == 0 else slots.at[s - 1]
+        src = total_buf if s == 0 else slots.at[s - 1]
         send, recv = (send_up, recv_up) if upward else (send_dn, recv_dn)
         lines = pl.ds(p * bit, bit)
         return pltpu.make_async_remote_copy(
@@ -330,12 +319,21 @@
     for p in range(PIECES):
         hop(0, p, True).start()
         hop(0, p, False).start()
+    firsts = compose(jnp.stack([gath[2], gath[4], twos[2]]), jnp.stack([twos[0], fours[0], fours[0]]))
+    gath[6] = compose(gath[6], firsts[2])
+    gath[1], gath[3] = twos[0], fours[0]
+    gath[2], gath[4], gath[5] = firsts[0], firsts[1], firsts[2]
+    gath[7] = total_buf[...]
     k_i, k_j = iota((K, 2 * K), 0), iota((K, 2 * K), 1)
     acc = jnp.where(k_i + K == k_j, 1.0, 0.0).astype(F32)
     state = jnp.zeros((K, K), F32)
     for s in range(n_up):
         if s == 0:
             lax.fori_loop(early, pairs, reaches, 0)
+        if s == n_up - 1:
+            prefix = gath[...]
+            near = mm3(prefix[:, :, K:].reshape(heads * K, K), acc).reshape(heads, K, 2 * K)
+            ready = jnp.concatenate([acc[None], near + place(prefix[:, :, :K])], axis=0)
         for p in range(PIECES):
             hop(s, p, True).wait_recv()
             if s + 1 < n_up:
@@ -345,19 +343,20 @@
                 if s + 1 < n_dn:
                     hop(s + 1, p, False).start()
         earlier = from_low[s]
+        if s == n_up - 1:
+            moved = mm3(earlier[:, K:], state) + earlier[:, :K]
+            state = jnp.where(z >= n_up, moved, state)
+            break
         joined = earlier if s == 0 else mm3(acc[:, K:], earlier) + place(acc[:, :K])
         acc = jnp.where(z >= s + 1, joined, acc)
         if s < n_dn:
             wrapped = from_high[s]
             moved = wrapped[:, :K] if s == 0 else mm3(wrapped[:, K:], state) + wrapped[:, :K]
             state = jnp.where(z + s + 1 >= planes, moved, state)
-    start = mm3(acc[:, K:], state) + acc[:, :K]
-
-    prefix = gath[...]
-    spread_out = mm3(prefix[:, :, K:].reshape(heads * K, K), start).reshape(heads, K, K) + prefix[:, :, :K]
-    out_buf[0] = start
-    out_buf[1:] = spread_out[:heads - 1]
-    end_buf[...] = spread_out[heads - 1]
+    spread_out = mm3(ready[:, :, K:].reshape((heads + 1) * K, K), state).reshape(heads + 1, K, K)
+    spread_out = spread_out + ready[:, :, :K]
+    out_buf[...] = spread_out[:heads]
+    end_buf[...] = spread_out[heads]
 
     def give_c(offset):
         other = peer(offset)
@@ -533,12 +532,11 @@
     n_up, n_dn = planes // 2, planes - 1 - planes // 2
     dma = pltpu.SemaphoreType.DMA
     vmem = pl.BlockSpec(memory_space=pltpu.VMEM)
-    outside = pl.BlockSpec(memory_space=pl.ANY)
     hbm = pl.BlockSpec(memory_space=pltpu.HBM)
     pair = (heads, K, 2 * K)
     return pl.pallas_call(
         functools.partial(whole_kernel, planes),
-        in_specs=[hbm, outside, outside, vmem, hbm],
+        in_specs=[vmem, vmem, vmem, vmem, hbm],
         out_specs=[vmem, vmem],
         out_shape=[
             jax.ShapeDtypeStruct((rows, columns), BF16),
@@ -546,13 +544,11 @@
         ],
         scratch_shapes=[
             pltpu.VMEM((K, K), F32),
-            pltpu.VMEM((heads // GROUP, 2, tokens, GROUP * K), BF16),
-            pltpu.VMEM((heads // GROUP, 2, tokens, GROUP * K), BF16),
-            pltpu.VMEM((tokens, wide), BF16),
             pltpu.VMEM((chunks, depth, width), BF16),
             pltpu.VMEM((tokens, 9 * heads), BF16),
             pltpu.VMEM((heads, nb * ROWS), F32),
             pltpu.VMEM(pair, F32),
+            pltpu.VMEM((K, 2 * K), F32),
             pltpu.VMEM(pair, F32),
             pltpu.VMEM((heads // GROUP, GROUP * nb, ROWS, 2 * K), BF16),
             pltpu.VMEM((heads // GROUP, GROUP * nb, ROWS, 2 * K), BF16),
@@ -572,7 +568,7 @@
             pltpu.VMEM((chunks, 4, rows, half), F32),
             pltpu.VMEM((heads, K, K), F32),
             pltpu.VMEM((planes - 1, K, K), F32),
-            dma((1,)), dma((heads // GROUP, GROUP, 2)), dma((chunks,)), dma((heads - 1,)), dma((heads,)),
+            dma((chunks,)), dma((heads - 1,)), dma((heads,)),
             dma((n_up, PIECES)), dma((n_up, PIECES)), dma((n_dn, PIECES)), dma((n_dn, PIECES)),
             dma((heads - 1,)), dma((heads,)),
             dma((chunks, 6)), dma((chunks, 2)), dma((chunks, 4)),
@@ -591,14 +587,14 @@
     heads = log_gate.shape[1]
     planes = lax.axis_size("seq") // heads
     tokens = queries.shape[0]
-    small = jnp.concatenate(
-        [
-            log_gate.T, beta_rates.T,
-            jnp.pad(norm_gain.reshape(1, K), ((0, 0), (0, tokens - K))),
-            jnp.pad(decode_owner.astype(F32), ((0, 0), (0, tokens - heads))),
-            jnp.zeros((5, tokens), F32),
-        ],
-        axis=0,
+    lines = 4 * heads
+
+    def laid(x, first):
+        return jnp.pad(x, ((first, lines - first - x.shape[0]), (0, tokens - x.shape[1])))
+
+    small = (
+        laid(log_gate.T, 0) + laid(beta_rates.T, heads) + laid(norm_gain.reshape(1, K), 3 * heads)
+        + laid(decode_owner, 3 * heads + 1).astype(F32)
     )
     return whole(
         queries, key_vectors.transpose(1, 0, 2), values.transpose(1, 0, 2), small, out_weight,

time: 96.9 us -> 93 us (0.960)
  local copies, waits for them, and re-layouts: 6.9 us -> 4.8 us
  Pallas kernels: 88.3 us -> 86.6 us
    pallas_call x1, Pallas kernels: 88.3 us -> 86.6 us  [whole(): pl.pallas_call(functools.partial(whole_kernel, planes), in_specs=[vmem, v...]
    concatenate x1 -> x0, local copies, waits for them, and re-layouts: 1.44 us -> none  [per_device(): jnp.concatenate([log_gate.T, beta_rates.T, jnp.pad(norm_gain.reshape(1, K...]
where the time goes in v5:
time: 93 us; the launch traced here: 92.8 us
  Pallas kernels  86.6 us (93%)
  local copies, waits for them, and re-layouts  4.8 us (5%)
    pallas_call x1, Pallas kernels, whole(): pl.pallas_call(functools.partial(whole_kernel, planes), in_specs=[vmem, v...  86.6 us
    unnamed x4, local copies, waits for them, and re-layouts  2.63 us
    transpose x1, local copies, waits for them, and re-layouts, per_device(): values.transpose(1, 0, 2)  2.18 us

profile of v5, /device:TPU:1, one launch (start us, length us, event | category | flops | bytes accessed | tf_op | source)
XLA Modules:
  0.0 92.8 jit_solution(3101716788571481530)
XLA Ops:
  0.6 0.8 convert_add_fusion.small_ref
  1.4 2.2 %copy_bitcast_fusion = (bf16[2,256,1024]{2,1,0:T(8,128)(2,1)S(1)}, bf16[2,256,1024]{2,1,0:T(8,128)(2,1)S(1)}) fusion(bf16[256,2,1024]{2,1,0:T(2,128)(2,1)} %param.10, bf16[256,2,1024]{2,1,0:T(2,128)(2,1)} %param.9), kind=kLoop, calls=%fused_computation | loop fusion | bytes 4194304 | tf_op jit(solution)/shard_map/transpose | solution.py:600
  3.6 0.0 copy-start
  3.6 1.0 %copy-done = bf16[256,1024]{1,0:T(8,128)(2,1)S(1)} copy-done((bf16[256,1024]{1,0:T(8,128)(2,1)S(1)}, bf16[256,1024]{1,0:T(8,128)(2,1)}, u32[]{:S(2)}) %copy-start) | copy-done | bytes 524312
  4.6 86.6 %whole.1 = (bf16[64,4096]{1,0:T(8,128)(2,1)S(1)}, f32[1,8,128,128]{3,2,1,0:T(8,128)S(1)}) custom-call(bf16[256,1024]{1,0:T(8,128)(2,1)S(1)} %copy-done, bf16[2,256,1024]{2,1,0:T(8,128)(2,1)S(1)} %get-tuple-element.3.k_ref, bf16[2,256,1024]{2,1,0:T(8,128)(2,1)S(1)} %get-tuple-element.2.v_ref, f32[32,256]{1,0:T(8,128)S(1)} %convert_add_fusion.small_ref, ...), custom_call_target="tpu_custom_call" | custom-call | tf_op jit(solution)/shard_map/whole/pallas_call | solution.py:537
  91.2 0.8 copy.16
  92.0 0.8 copy.17
Async XLA Ops:
  3.6 1.0 %copy-start = (bf16[256,1024]{1,0:T(8,128)(2,1)S(1)}, bf16[256,1024]{1,0:T(8,128)(2,1)}, u32[]{:S(2)}) copy-start(bf16[256,1024]{1,0:T(8,128)(2,1)} %q_buf.1) | copy-start | bytes 1572868

commit v6 on v5

--- a/solution.py
+++ b/solution.py
@@ -48,7 +48,7 @@
 
 
 MESH = pl.DeviceIdType.MESH
-PIECES = 2
+PIECES = 4
 GROUP = 4
 
 
@@ -277,7 +277,7 @@
         h0 = pair
         (run,) = columns(h0, (2,))
         query = by_head(q_buf, h0)
-        scores = mm3(query, (kt_hi[pair], kt_lo[pair])) * decays(run, lane_rows(h0))
+        scores = twin(query, (kt_hi[pair], kt_lo[pair])) * decays(run, lane_rows(h0))
         z_out = mm3(scores, (rows_hi[pair], rows_lo[pair])).reshape(GROUP, nb, TB, 2 * K)
         reach = (jnp.exp(run) * query).reshape(GROUP, nb, TB, K) - z_out[..., K:]
         base = [z_out[:, 0, :, :K]]
@@ -523,7 +523,7 @@
             hop(s, p, False).wait_send()
 
 
-def whole(queries, keys, vals, small, out_weight, heads, planes, ring, chunks=8):
+def whole(queries, keys, vals, small, out_weight, heads, planes, ring, chunks=4):
     tokens, wide = queries.shape
     nb = tokens // TB
     depth, columns = out_weight.shape

time: 93 us -> 92.6 us (level)
  no operation moved by 1% of the time
where the time goes in v6:
time: 92.6 us; the launch traced here: 92.4 us
  Pallas kernels  86.1 us (93%)
  local copies, waits for them, and re-layouts  4.8 us (5%)
    pallas_call x1, Pallas kernels, whole(): pl.pallas_call(functools.partial(whole_kernel, planes), in_specs=[vmem, v...  86.1 us
    unnamed x4, local copies, waits for them, and re-layouts  2.63 us
    transpose x1, local copies, waits for them, and re-layouts, per_device(): values.transpose(1, 0, 2)  2.18 us

profile of v6, /device:TPU:1, one launch (start us, length us, event | category | flops | bytes accessed | tf_op | source)
XLA Modules:
  0.0 92.4 jit_solution(14725124675615591528)
XLA Ops:
  0.6 0.8 convert_add_fusion.small_ref
  1.4 2.2 %copy_bitcast_fusion = (bf16[2,256,1024]{2,1,0:T(8,128)(2,1)S(1)}, bf16[2,256,1024]{2,1,0:T(8,128)(2,1)S(1)}) fusion(bf16[256,2,1024]{2,1,0:T(2,128)(2,1)} %param.10, bf16[256,2,1024]{2,1,0:T(2,128)(2,1)} %param.9), kind=kLoop, calls=%fused_computation | loop fusion | bytes 4194304 | tf_op jit(solution)/shard_map/transpose | solution.py:600
  3.6 0.0 copy-start
  3.6 1.0 %copy-done = bf16[256,1024]{1,0:T(8,128)(2,1)S(1)} copy-done((bf16[256,1024]{1,0:T(8,128)(2,1)S(1)}, bf16[256,1024]{1,0:T(8,128)(2,1)}, u32[]{:S(2)}) %copy-start) | copy-done | bytes 524312
  4.6 86.1 %whole.1 = (bf16[64,4096]{1,0:T(8,128)(2,1)S(1)}, f32[1,8,128,128]{3,2,1,0:T(8,128)S(1)}) custom-call(bf16[256,1024]{1,0:T(8,128)(2,1)S(1)} %copy-done, bf16[2,256,1024]{2,1,0:T(8,128)(2,1)S(1)} %get-tuple-element.3.k_ref, bf16[2,256,1024]{2,1,0:T(8,128)(2,1)S(1)} %get-tuple-element.2.v_ref, f32[32,256]{1,0:T(8,128)S(1)} %convert_add_fusion.small_ref, ...), custom_call_target="tpu_custom_call" | custom-call | tf_op jit(solution)/shard_map/whole/pallas_call | solution.py:537
  90.8 0.8 copy.16
  91.6 0.8 copy.17
Async XLA Ops:
  3.6 1.0 %copy-start = (bf16[256,1024]{1,0:T(8,128)(2,1)S(1)}, bf16[256,1024]{1,0:T(8,128)(2,1)}, u32[]{:S(2)}) copy-start(bf16[256,1024]{1,0:T(8,128)(2,1)} %q_buf.1) | copy-start | bytes 1572868

commit v7 on v6

--- a/solution.py
+++ b/solution.py
@@ -118,7 +118,7 @@
 def whole_kernel(
     planes, q_buf, k_ref, v_ref, small_ref, w_ref,
     out_ref, states_ref, taken, w_buf, col_scr, row_scr, sp, total_buf, gath, rows_hi, rows_lo,
-    kt_hi, kt_lo, carry, reach_scr, base_scr, from_low, from_high, out_buf, in_buf, end_buf,
+    kt_hi, kt_lo, carry, reach_hi, reach_lo, base_scr, from_low, from_high, out_buf, in_buf, end_buf,
     normed, part, relay, landed, finals, chosen,
     w_sem, send_a, recv_a, send_up, recv_up, send_dn, recv_dn, send_c, recv_c,
     send_sem, relay_sem, land_sem, share_send, share_recv, give_send, give_recv,
@@ -287,7 +287,7 @@
             base.append(both[:, :, :K] + z_out[:, b, :, :K])
             whole_reach.append(both[:, :, K:])
         base_scr[pair] = jnp.concatenate(base, axis=1)
-        reach_scr[pair] = jnp.concatenate(whole_reach, axis=1)
+        reach_hi[pair], reach_lo[pair] = split(jnp.concatenate(whole_reach, axis=1))
         return 0
 
     early = jnp.where(lax.rem(i, pairs) == 0, 0, pairs)
@@ -405,7 +405,7 @@
                 here = in_buf.at[step, g]
                 pltpu.make_async_copy(here, here, recv_c.at[h]).wait()
 
-        attended = base_scr[step] + mm3(reach_scr[step], in_buf[step])
+        attended = base_scr[step] + mm3((reach_hi[step], reach_lo[step]), in_buf[step])
         scale = lax.rsqrt(jnp.mean(attended * attended, axis=-1, keepdims=True) + 1e-6)
         got = (attended * scale * gain).astype(BF16)
         for g in range(GROUP):
@@ -555,7 +555,8 @@
             pltpu.VMEM((heads // GROUP, GROUP * nb, K, ROWS), BF16),
             pltpu.VMEM((heads // GROUP, GROUP * nb, K, ROWS), BF16),
             pltpu.VMEM((heads // GROUP, nb - 1, GROUP, K, 2 * K), F32),
-            pltpu.VMEM((heads // GROUP, GROUP, tokens, K), F32),
+            pltpu.VMEM((heads // GROUP, GROUP, tokens, K), BF16),
+            pltpu.VMEM((heads // GROUP, GROUP, tokens, K), BF16),
             pltpu.VMEM((heads // GROUP, GROUP, tokens, K), F32),
             pltpu.VMEM((n_up, K, 2 * K), F32),
             pltpu.VMEM((n_dn, K, 2 * K), F32),

time: 92.6 us -> 92.6 us (level)
  no operation moved by 1% of the time
where the time goes in v7:
time: 92.6 us; the launch traced here: 92.4 us
  Pallas kernels  86.1 us (93%)
  local copies, waits for them, and re-layouts  4.8 us (5%)
    pallas_call x1, Pallas kernels, whole(): pl.pallas_call(functools.partial(whole_kernel, planes), in_specs=[vmem, v...  86.1 us
    unnamed x4, local copies, waits for them, and re-layouts  2.63 us
    transpose x1, local copies, waits for them, and re-layouts, per_device(): values.transpose(1, 0, 2)  2.18 us

profile of v7, /device:TPU:1, one launch (start us, length us, event | category | flops | bytes accessed | tf_op | source)
XLA Modules:
  0.0 92.4 jit_solution(11067400450134780365)
XLA Ops:
  0.6 0.8 convert_add_fusion.small_ref
  1.4 2.2 %copy_bitcast_fusion = (bf16[2,256,1024]{2,1,0:T(8,128)(2,1)S(1)}, bf16[2,256,1024]{2,1,0:T(8,128)(2,1)S(1)}) fusion(bf16[256,2,1024]{2,1,0:T(2,128)(2,1)} %param.10, bf16[256,2,1024]{2,1,0:T(2,128)(2,1)} %param.9), kind=kLoop, calls=%fused_computation | loop fusion | bytes 4194304 | tf_op jit(solution)/shard_map/transpose | solution.py:601
  3.6 0.0 copy-start
  3.6 1.0 %copy-done = bf16[256,1024]{1,0:T(8,128)(2,1)S(1)} copy-done((bf16[256,1024]{1,0:T(8,128)(2,1)S(1)}, bf16[256,1024]{1,0:T(8,128)(2,1)}, u32[]{:S(2)}) %copy-start) | copy-done | bytes 524312
  4.6 86.1 %whole.1 = (bf16[64,4096]{1,0:T(8,128)(2,1)S(1)}, f32[1,8,128,128]{3,2,1,0:T(8,128)S(1)}) custom-call(bf16[256,1024]{1,0:T(8,128)(2,1)S(1)} %copy-done, bf16[2,256,1024]{2,1,0:T(8,128)(2,1)S(1)} %get-tuple-element.3.k_ref, bf16[2,256,1024]{2,1,0:T(8,128)(2,1)S(1)} %get-tuple-element.2.v_ref, f32[32,256]{1,0:T(8,128)S(1)} %convert_add_fusion.small_ref, ...), custom_call_target="tpu_custom_call" | custom-call | tf_op jit(solution)/shard_map/whole/pallas_call | solution.py:537
  90.8 0.8 copy.16
  91.6 0.8 copy.17
Async XLA Ops:
  3.6 1.0 %copy-start = (bf16[256,1024]{1,0:T(8,128)(2,1)S(1)}, bf16[256,1024]{1,0:T(8,128)(2,1)}, u32[]{:S(2)}) copy-start(bf16[256,1024]{1,0:T(8,128)(2,1)} %q_buf.1) | copy-start | bytes 1572868
